TPU v7x, 32 devices: a whole 2x2x4 slice. The times are simulated.
32 devices in a mesh: col: 4 (over x, core), row: 8 (over z, y).
Axes of the slice: x: 2, y: 2, z: 4, core: 2. Of those that a mesh axis runs over, the one named last changes fastest.
Arguments:
- features: float32 [4096, 512], P(('row', 'col')), may hold values from -6 to 6
- weight: float32 [512, 512], replicated, may hold values from -0.25 to 0.25
- tiles: bfloat16 [4, 8, 6, 128, 128], P('col', 'row'), may hold values from -0.1875 to 0.1875
- tile_rows: int32 [4, 8, 6], P('col', 'row'), may hold values from 0 to 7, as said below
- tile_cols: int32 [4, 8, 6], P('col', 'row'), may hold values from 0 to 3
- tile_count: int32 [4, 8], P('col', 'row'), may hold values from 1 to 6, as said below
- cotangent: bfloat16 [4096, 512], P(('col', 'row')), may hold values from -6 to 6
Outputs:
- aggregated: bfloat16 [4096, 512], P(('col', 'row'))
- grad_x: float32 [4096, 512], P(('row', 'col'))
- grad_w: float32 [512, 512], replicated
Inputs may be any that keep to these rules, and one draw needn't show every extreme that they name: `tile_rows`: within one grid block the live slots name distinct tiles. `tile_count`: some grid block has all 6 slots live.
All inputs are finite; a program needn't handle non-finite values.
Results may differ from a plain program's by a relative error of at most 0.0049.
Values may be sent and summed in bfloat16 or wider, within the bound.
A program may use at most 128 MiB of HBM per device.

v0:
```python
import jax
import jax.numpy as jnp
from jax import lax
from jax.sharding import PartitionSpec as P


def shards(features, weight, tiles, tile_rows, tile_cols, tile_count, cotangent):
    tile_size = tiles.shape[-1]
    slot_count = tiles.shape[2]
    feat_width = features.shape[1]
    blocks = tiles[0, 0]
    rows_idx = tile_rows[0, 0]
    cols_idx = tile_cols[0, 0]
    live_slots = jnp.arange(slot_count, dtype=jnp.int32) < tile_count[0, 0]
    local_rows = jnp.dot(
        features, weight, precision=lax.Precision.HIGHEST, preferred_element_type=jnp.float32
    ).astype(jnp.bfloat16)
    source = lax.all_gather(local_rows, "col", axis=0, tiled=True)
    source_tiles = source.reshape(-1, tile_size, feat_width)
    src_count = source_tiles.shape[0]
    out_tiles = lax.axis_size("row") * features.shape[0] // tile_size
    picked = jnp.take(source_tiles, cols_idx, axis=0)
    tile_terms = jnp.einsum("tab,tbf->taf", blocks, picked, preferred_element_type=jnp.float32)
    select_dst = (
        (rows_idx[None, :] == jnp.arange(out_tiles, dtype=jnp.int32)[:, None]) & live_slots[None, :]
    ).astype(jnp.float32)
    partial_value = jnp.einsum(
        "it,taf->iaf", select_dst, tile_terms, precision=lax.Precision.HIGHEST
    )
    partial_value = partial_value.reshape(out_tiles * tile_size, feat_width)
    aggregated = lax.psum_scatter(partial_value, "row", scatter_dimension=0, tiled=True).astype(
        jnp.bfloat16
    )
    gathered = lax.all_gather(cotangent, "row", axis=0, tiled=True)
    grad_tiles = gathered.reshape(out_tiles, tile_size, feat_width)
    picked_grad = jnp.take(grad_tiles, rows_idx, axis=0)
    back_terms = jnp.einsum("tab,taf->tbf", blocks, picked_grad, preferred_element_type=jnp.float32)
    select_src = (
        (cols_idx[None, :] == jnp.arange(src_count, dtype=jnp.int32)[:, None]) & live_slots[None, :]
    ).astype(jnp.float32)
    back_partial = jnp.einsum(
        "kt,tbf->kbf", select_src, back_terms, precision=lax.Precision.HIGHEST
    )
    back_partial = back_partial.reshape(src_count * tile_size, feat_width)
    grad_y = lax.psum_scatter(back_partial, "col", scatter_dimension=0, tiled=True)
    grad_x = jnp.dot(
        grad_y, weight.T, precision=lax.Precision.HIGHEST, preferred_element_type=jnp.float32
    )
    weight_terms = jnp.dot(
        features.T, grad_y, precision=lax.Precision.HIGHEST, preferred_element_type=jnp.float32
    )
    grad_w = lax.psum(weight_terms, ("col", "row"))
    return (aggregated, grad_x, grad_w)


def solution(mesh):
    placed = (
        P(("row", "col"), None),
        P(),
        P("col", "row", None, None, None),
        P("col", "row", None),
        P("col", "row", None),
        P("col", "row"),
        P(("col", "row"), None),
    )
    return jax.shard_map(
        shards,
        mesh=mesh,
        in_specs=placed,
        out_specs=(P(("col", "row"), None), P(("row", "col"), None), P()),
        check_vma=False,
    )
```

profile of v0, /device:TPU:1, one launch (start us, length us, event | category | flops | bytes accessed | tf_op | source)
XLA Modules:
  0.0 300.5 jit_solution(10437978036787371272)
XLA Ops:
  7.2 0.0 copy-start
  7.2 0.0 all-gather.2.cloned.1.call-start
  7.2 0.7 all-gather.2.cloned.1.call-update
  7.9 0.0 reduce-scatter.5.cloned.1.call-start
  8.6 0.7 fusion.25
  9.3 0.7 compare_and_fusion
  9.9 41.5 %all-gather.2.cloned.1.call-done = bf16[1024,512]{1,0:T(8,128)(2,1)} async-done(((bf16[128,512]{1,0:T(8,128)(2,1)}), bf16[1024,512]{1,0:T(8,128)(2,1)}) %all-gather.2.cloned.1.call-update) | async-done | bytes 1048592 | tf_op jit(solution)/shard_map/all_gather | solution.py:34
  51.4 1.8 gather_fusion.1
  53.2 2.6 fusion.4
  55.8 0.0 copy-start.4
  55.8 2.2 copy.15
  58.0 0.0 copy-done.4
  58.0 1.1 fusion
  59.1 0.0 copy-start.1
  59.1 1.3 copy.12
  60.4 0.0 reduce-scatter.5.cloned.1.call-update
  60.4 0.0 copy-start.3
  60.4 0.0 reduce-scatter.3.cloned.1.call-start
  60.5 0.0 copy-done
  60.5 0.0 copy-done.1
  60.5 0.7 convolution_convert_fusion
  61.2 8.7 %all_gather.6 = bf16[512,512]{1,0:T(8,128)(2,1)S(1)} all-gather(bf16[128,512]{1,0:T(8,128)(2,1)S(1)} %convolution_convert_fusion), channel_id=1, replica_groups=mesh['col'=4,'row'=8] {'col'}, dimensions={0}, use_global_device_ids=true | all-gather | bytes 655360 | tf_op jit(solution)/shard_map/all_gather | solution.py:18
  69.9 0.6 gather_fusion
  70.5 0.0 copy-done.3
  70.5 1.7 fusion.6
  72.2 0.0 copy-start.5
  72.2 2.2 copy.14
  74.3 0.0 copy-done.5
  74.4 1.1 fusion.2
  75.5 2.6 copy.11
  78.0 0.0 reduce-scatter.3.cloned.1.call-update
  78.1 0.0 all-reduce.2.cloned.1.call-start
  78.1 7.1 %reduce-scatter.5.cloned.1.call-done = f32[128,512]{1,0:T(8,128)} async-done(((f32[512,512]{1,0:T(8,128)}), f32[128,512]{1,0:T(8,128)}) %reduce-scatter.5.cloned.1.call-update) | async-done | bytes 262160 | tf_op jit(solution)/shard_map/reduce_scatter | solution.py:45
  85.2 0.0 copy-start.2
  85.2 3.0 %convolution_bitcast_fusion = f32[512,512]{0,1:T(8,128)} fusion(f32[128,512]{1,0:T(8,128)} %reduce-scatter.5.cloned.1.call-done, f32[128,512]{1,0:T(8,128)S(1)} %copy-done.1), kind=kOutput, calls=%fused_computation.6 | convolution fusion | flops 402653184 | bytes 1572864 | tf_op jit(solution)/shard_map/dot_general | solution.py:49
  88.2 0.0 all-reduce.2.cloned.1.call-update
  88.3 0.0 copy-done.2
  88.3 1.9 fusion.28
  90.2 65.0 %reduce-scatter.3.cloned.1.call-done = f32[128,512]{1,0:T(8,128)} async-done(((f32[1024,512]{1,0:T(8,128)}), f32[128,512]{1,0:T(8,128)}) %reduce-scatter.3.cloned.1.call-update) | async-done | bytes 262160 | tf_op jit(solution)/shard_map/reduce_scatter | solution.py:31
  155.1 1.6 convert_element_type.9
  156.8 134.6 %all-reduce.2.cloned.1.call-done = f32[512,512]{0,1:T(8,128)} async-done(((f32[512,512]{0,1:T(8,128)}), f32[512,512]{0,1:T(8,128)}) %all-reduce.2.cloned.1.call-update) | async-done | bytes 1048592 | tf_op jit(solution)/shard_map/psum | solution.py:52
  291.4 2.5 copy.13
  (5 shorter events, 0.0 us)
Async XLA Ops:
  7.2 53.3 %copy-start = (f32[512,512]{1,0:T(8,128)S(1)}, f32[512,512]{1,0:T(8,128)}, u32[]{:S(2)}) copy-start(f32[512,512]{1,0:T(8,128)} %param.8) | copy-start | bytes 3145732
  7.2 44.2 %all-gather.2.cloned.1.call-start = ((), (), s32[]{:S(2)}) async-start(), calls=%async_computation.3 | async-start | bytes 1179648 | tf_op jit(solution)/shard_map/all_gather | solution.py:34
  7.9 77.3 %reduce-scatter.5.cloned.1.call-start = ((), (), s32[]{:S(2)}) async-start(), calls=%async_computation.4 | async-start | bytes 1310720 | tf_op jit(solution)/shard_map/reduce_scatter | solution.py:45
  55.8 2.2 copy-start.4
  59.1 1.4 copy-start.1
  60.4 10.1 %copy-start.3 = (bf16[1,1,6,128,128]{4,3,2,1,0:T(8,128)(2,1)S(1)}, bf16[1,1,6,128,128]{4,3,2,1,0:T(8,128)(2,1)}, u32[]{:S(2)}) copy-start(bf16[1,1,6,128,128]{4,3,2,1,0:T(8,128)(2,1)} %param.9) | copy-start | bytes 589828
  60.4 94.7 %reduce-scatter.3.cloned.1.call-start = ((), (), s32[]{:S(2)}) async-start(), calls=%async_computation.2 | async-start | bytes 2359296 | tf_op jit(solution)/shard_map/reduce_scatter | solution.py:31
  72.2 2.2 copy-start.5
  78.1 213.4 %all-reduce.2.cloned.1.call-start = ((), (), s32[]{:S(2)}) async-start(), calls=%async_computation.5 | async-start | bytes 2097152 | tf_op jit(solution)/shard_map/psum | solution.py:52
  85.2 3.0 %copy-start.2 = (f32[128,512]{1,0:T(8,128)S(1)}, f32[128,512]{1,0:T(8,128)}, u32[]{:S(2)}) copy-start(f32[128,512]{1,0:T(8,128)} %reduce-scatter.5.cloned.1.call-done) | copy-start | bytes 786436
Sparse Core Ops, SparseCore 0:
  10.1 41.2 all-gather.1
  60.5 24.6 reduce-scatter.4
  89.2 65.9 reduce-scatter.2
  161.6 129.7 all-reduce.1
where the time goes:
time: 302 us; the launch traced here: 300 us
  waiting for transfers between devices  249 us (82%)
  between operations  14.6 us (5%)
  local copies, waits for them, and re-layouts  13.1 us (4%)
  matrix products  12 us (4%)
  blocking collectives  8.66 us (3%)
    psum x1, waiting for transfers between devices, shards(): grad_w = lax.psum(weight_terms, ('col', 'row'))  135 us
    reduce_scatter x1, waiting for transfers between devices, shards(): lax.psum_scatter(partial_value, 'row', scatter_dimension=0, tiled=True)  65 us
    all_gather x1, waiting for transfers between devices, shards(): gathered = lax.all_gather(cotangent, 'row', axis=0, tiled=True)  41.5 us
    all_gather x1, blocking collectives, shards(): source = lax.all_gather(local_rows, 'col', axis=0, tiled=True)  8.66 us
    reduce_scatter x1, waiting for transfers between devices, shards(): lax.psum_scatter(back_partial, 'col', scatter_dimension=0, tiled=True)  7.11 us
  transfers between devices with their start and end apart: 4, of which 4 were waited for; matrix products, arithmetic and copies ran while one was open for 6% of the time, Pallas kernels for 0%

commit v1 on v0

v1 whole, which is shorter than its diff:
```python
import functools

import jax
import jax.numpy as jnp
from jax import lax
from jax.experimental import pallas as pl
from jax.experimental.pallas import tpu as pltpu
from jax.sharding import PartitionSpec as P

BF16 = jnp.bfloat16
F32 = jnp.float32
MESH = pl.DeviceIdType.MESH


def each(count, body):
    if count <= 8:
        for step in range(count):
            body(step)
    else:
        lax.fori_loop(0, count, lambda step, _: (body(step), None)[1], None)


def matmul(a, b, contract=((1,), (0,))):
    return lax.dot_general(a, b, (contract, ((), ())), preferred_element_type=F32)


def layer_kernel(
    n_col, n_row, inner, pieces,
    rows_ref, cols_ref, count_ref, feat_ref, w_ref, tiles_ref, cot_ref,
    agg_ref, gx_ref, gw_ref,
    feat_all, cot_all, pad, pad_t, a_ref, at_ref, w_hi, w_lo, proj, part, part_send, y_in, z_in,
    back, back_send, c_in, g_part, g1_in, g1_sum, g2_in, gw_all,
    feat_s, feat_r, cotz_s, coty_s, cot_r, py_s, py_r, pz_s, pz_r, c_s, c_r,
    g1_s, g1_r, g2_s, g2_r, g3_s, g3_r, g4_s, g4_r,
):
    outer = n_row // inner
    slots, tile = tiles_ref.shape[0], tiles_ref.shape[1]
    rows_dev, width = cot_ref.shape
    per_dev = rows_dev // tile
    dst_tiles, src_tiles = n_row * per_dev, n_col * per_dev
    col, row = lax.axis_index("col"), lax.axis_index("row")
    out_id, in_id = row // inner, row % inner
    g_rows = width // n_col
    g_piece = g_rows // pieces

    def send(src, dst, s_sem, r_sem, target):
        copy = pltpu.make_async_remote_copy(
            src_ref=src, dst_ref=dst, send_sem=s_sem, recv_sem=r_sem,
            device_id=target, device_id_type=MESH,
        )
        copy.start()

    def sent(ref, s_sem):
        pltpu.make_async_remote_copy(
            src_ref=ref, dst_ref=ref, send_sem=s_sem, recv_sem=s_sem,
            device_id={"col": col}, device_id_type=MESH,
        ).wait_send()

    def landed(ref, r_sem):
        pltpu.make_async_remote_copy(
            src_ref=ref, dst_ref=ref, send_sem=r_sem, recv_sem=r_sem,
            device_id={"col": col}, device_id_type=MESH,
        ).wait_recv()

    def col_at(d):
        return lax.rem(col + d, n_col)

    def row_at(d):
        return lax.rem(row + d, n_row)

    def out_at(d):
        return lax.rem(out_id + d, outer)

    def in_at(d):
        return lax.rem(in_id + d, inner)

    def reducer(r, body):
        if pieces == n_row:
            body()
        else:
            pl.when(r < pieces)(body)

    barrier = pltpu.get_barrier_semaphore()
    each(n_col - 1, lambda d: pl.semaphore_signal(
        barrier, inc=1, device_id={"col": col_at(d + 1)}, device_id_type=MESH))
    each(n_row - 1, lambda d: pl.semaphore_signal(
        barrier, inc=1, device_id={"row": row_at(d + 1)}, device_id_type=MESH))
    feat_all[col] = feat_ref[...].astype(BF16)
    cot_all[row] = cot_ref[...]
    pl.semaphore_wait(barrier, n_col + n_row - 2)

    def cot_out(d):
        send(cot_ref, cot_all.at[row], cotz_s.at[d], cot_r.at[row], {"row": out_at(d + 1) * inner + in_id})

    def cot_forward(o, d_out):
        def one(d):
            slot = o * inner + in_id
            send(cot_all.at[slot], cot_all.at[slot], coty_s.at[d_out, d], cot_r.at[slot],
                 {"row": out_id * inner + in_at(d + 1)})
        each(inner - 1, one)

    each(outer - 1, cot_out)
    cot_forward(out_id, 0)

    def feat_out(d):
        send(feat_all.at[col], feat_all.at[col], feat_s.at[d], feat_r.at[col], {"col": col_at(d + 1)})

    each(n_col - 1, feat_out)

    def pad_one(t):
        one = tiles_ref[t]
        pad[t] = one
        pad_t[t] = one.T

    each(slots, pad_one)
    pad[slots] = jnp.zeros((tile, tile), BF16)
    pad_t[slots] = jnp.zeros((tile, tile), BF16)
    live = count_ref[0]
    places = [
        jnp.where(t < live, rows_ref[t] * src_tiles + cols_ref[t], -1) for t in range(slots)
    ]

    def lay(i):
        for k in range(src_tiles):
            index = jnp.int32(slots)
            for t in range(slots):
                index = jnp.where(places[t] == i * src_tiles + k, t, index)
            at = i * tile if isinstance(i, int) else pl.multiple_of(i * tile, tile)
            a_ref[pl.ds(at, tile), k * tile:(k + 1) * tile] = pad[index]
            at_ref[k * tile:(k + 1) * tile, pl.ds(at, tile)] = pad_t[index]

    each(dst_tiles, lay)
    weight = w_ref[...]
    w_hi[...] = weight.astype(BF16)
    w_lo[...] = (weight - w_hi[...].astype(F32)).astype(BF16)

    def project(d):
        c = col_at(d)
        if not (isinstance(d, int) and d == 0):
            landed(feat_all.at[c], feat_r.at[c])
        block = feat_all[c]
        proj[pl.ds(pl.multiple_of(c * rows_dev, rows_dev), rows_dev), :] = (
            matmul(block, w_hi[...]) + matmul(block, w_lo[...])
        ).astype(BF16)

    project(0)
    each(n_col - 1, lambda d: project(d + 1))

    def pass_on(d):
        o = out_at(d + 1)
        landed(cot_all.at[o * inner + in_id], cot_r.at[o * inner + in_id])
        cot_forward(o, d + 1)

    each(outer - 1, pass_on)

    def forward(d):
        o = out_at(d + 1)
        span = inner * rows_dev
        block = a_ref[pl.ds(pl.multiple_of(o * span, span), span), :]
        result = matmul(block, proj[...]).reshape(inner, rows_dev, width)
        part[o] = result
        part_send[o] = result.astype(BF16)

        def one(e):
            target = in_at(e + 1)
            send(part_send.at[o, target], y_in.at[o, in_id], py_s.at[o, e], py_r.at[o, in_id],
                 {"row": out_id * inner + target})
        each(inner - 1, one)

    each(outer, forward)

    def backward(d):
        o = out_at(d)
        span = inner * rows_dev

        def one(e):
            slot = o * inner + in_at(e + 1)
            landed(cot_all.at[slot], cot_r.at[slot])
        each(inner - 1, one)
        block = at_ref[:, pl.ds(pl.multiple_of(o * span, span), span)]
        cots = cot_all[pl.ds(o * inner, inner)].reshape(span, width)
        term = matmul(block, cots)
        if isinstance(d, int) and d == 0:
            back[...] = term
        else:
            back[...] += term

    backward(0)
    each(outer - 1, lambda d: backward(d + 1))
    back_send[...] = back[...].astype(BF16).reshape(n_col, rows_dev, width)

    g_part[...] = matmul(
        feat_all[...].reshape(n_col * rows_dev, width),
        back_send[...].reshape(n_col * rows_dev, width),
        ((0,), (0,)),
    ).astype(BF16).reshape(n_col, g_rows, width)

    def g1_out(d):
        c = col_at(d + 1)
        send(g_part.at[c], g1_in.at[col], g1_s.at[d], g1_r.at[col], {"col": c})

    def c_out(d):
        c = col_at(d + 1)
        send(back_send.at[c], c_in.at[col], c_s.at[d], c_r.at[col], {"col": c})

    each(n_col - 1, g1_out)
    each(n_col - 1, c_out)

    def inner_sum(o):
        def one(e):
            source = in_at(e + 1)
            landed(y_in.at[o, source], py_r.at[o, source])
            part[o, in_id] += y_in[o, source].astype(F32)
        each(inner - 1, one)

    def outer_out(d):
        o = out_at(d + 1)
        inner_sum(o)
        part_send[o, in_id] = part[o, in_id].astype(BF16)
        send(part_send.at[o, in_id], z_in.at[out_id], pz_s.at[d], pz_r.at[out_id], {"row": o * inner + in_id})

    each(outer - 1, outer_out)
    inner_sum(out_id)

    gw_part = g_part[col].astype(F32)
    def g1_add(d, total):
        c = col_at(d + 1)
        landed(g1_in.at[c], g1_r.at[c])
        return total + g1_in[c].astype(F32)
    for d in range(n_col - 1):
        gw_part = g1_add(d, gw_part)
    g1_sum[...] = gw_part.astype(BF16).reshape(pieces, g_piece, width)

    def g2_out(d):
        r = row_at(d + 1)
        reducer(r, lambda: send(g1_sum.at[r], g2_in.at[row], g2_s.at[d], g2_r.at[row], {"row": r}))

    each(n_row - 1, g2_out)

    def c_add(d):
        c = col_at(d + 1)
        landed(c_in.at[c], c_r.at[c])
    each(n_col - 1, c_add)
    grad_y = back[pl.ds(pl.multiple_of(col * rows_dev, rows_dev), rows_dev), :]
    for d in range(n_col - 1):
        grad_y = grad_y + c_in[col_at(d + 1)].astype(F32)
    grad_y = grad_y.astype(BF16)
    gx_ref[...] = matmul(grad_y, w_hi[...], ((1,), (1,))) + matmul(grad_y, w_lo[...], ((1,), (1,)))

    def g2_sum():
        def g2_wait(d):
            r = row_at(d + 1)
            landed(g2_in.at[r], g2_r.at[r])
        each(n_row - 1, g2_wait)
        g2_in[row] = g1_sum[row]
        total = g2_in[0].astype(F32)
        for r in range(1, n_row):
            total = total + g2_in[r].astype(F32)
        gw_all[col, row] = total.astype(BF16)

        def g3_out(d):
            send(gw_all.at[col, row], gw_all.at[col, row], g3_s.at[d], g3_r.at[row], {"row": row_at(d + 1)})
        each(n_row - 1, g3_out)

    reducer(row, g2_sum)

    def z_wait(d):
        o = out_at(d + 1)
        landed(z_in.at[o], pz_r.at[o])
        part[out_id, in_id] += z_in[o].astype(F32)

    each(outer - 1, z_wait)
    agg_ref[...] = part[out_id, in_id].astype(BF16)

    def g3_wait(d):
        r = row_at(d + 1)
        reducer(r, lambda: landed(gw_all.at[col, r], g3_r.at[r]))

    each(n_row - 1, g3_wait)

    def g4_out(d):
        send(gw_all.at[col], gw_all.at[col], g4_s.at[d], g4_r.at[col], {"col": col_at(d + 1)})

    each(n_col - 1, g4_out)

    def g4_wait(d):
        c = col_at(d + 1)
        landed(gw_all.at[c], g4_r.at[c])
        gw_ref[pl.ds(pl.multiple_of(c * g_rows, g_rows), g_rows), :] = (
            gw_all[c].reshape(g_rows, width).astype(F32))

    gw_ref[pl.ds(pl.multiple_of(col * g_rows, g_rows), g_rows), :] = (
        gw_all[col].reshape(g_rows, width).astype(F32))
    each(n_col - 1, g4_wait)

    each(n_col - 1, lambda d: sent(feat_all.at[0], feat_s.at[d]))
    each(outer - 1, lambda d: sent(cot_ref, cotz_s.at[d]))
    each(outer, lambda d: each(inner - 1, lambda e: sent(cot_ref, coty_s.at[d, e])))
    each(outer, lambda d: each(inner - 1, lambda e: sent(y_in.at[0, 0], py_s.at[d, e])))
    each(outer - 1, lambda d: sent(z_in.at[0], pz_s.at[d]))
    each(n_col - 1, lambda d: sent(c_in.at[0], c_s.at[d]))
    each(n_col - 1, lambda d: sent(g1_in.at[0], g1_s.at[d]))
    each(n_row - 1, lambda d: reducer(row_at(d + 1), lambda: sent(g2_in.at[0], g2_s.at[d])))
    reducer(row, lambda: each(n_row - 1, lambda d: sent(g2_in.at[0], g3_s.at[d])))
    each(n_col - 1, lambda d: sent(gw_all.at[0], g4_s.at[d]))


def shards(n_col, n_row, features, weight, tiles, tile_rows, tile_cols, tile_count, cotangent):
    slots, tile = tiles.shape[2], tiles.shape[-1]
    rows_dev, width = features.shape
    inner = 2 if n_row % 2 == 0 else 1
    outer = n_row // inner
    g_rows = width // n_col
    pieces = min(n_row, g_rows // 16)
    g_piece = g_rows // pieces
    src, dst = n_col * rows_dev, n_row * rows_dev
    dma = pltpu.SemaphoreType.DMA
    vmem = pl.BlockSpec(memory_space=pltpu.VMEM)
    smem = pl.BlockSpec(memory_space=pltpu.SMEM)
    buffers = [
        ((n_col, rows_dev, width), BF16),
        ((n_row, rows_dev, width), BF16),
        ((slots + 1, tile, tile), BF16),
        ((slots + 1, tile, tile), BF16),
        ((dst, src), BF16),
        ((src, dst), BF16),
        ((width, width), BF16),
        ((width, width), BF16),
        ((src, width), BF16),
        ((outer, inner, rows_dev, width), F32),
        ((outer, inner, rows_dev, width), BF16),
        ((outer, inner, rows_dev, width), BF16),
        ((outer, rows_dev, width), BF16),
        ((src, width), F32),
        ((n_col, rows_dev, width), BF16),
        ((n_col, rows_dev, width), BF16),
        ((n_col, g_rows, width), BF16),
        ((n_col, g_rows, width), BF16),
        ((pieces, g_piece, width), BF16),
        ((n_row, g_piece, width), BF16),
        ((n_col, pieces, g_piece, width), BF16),
    ]
    sems = [
        (n_col,), (n_col,), (outer,), (outer, inner), (n_row,), (outer, inner), (outer, inner),
        (outer,), (outer,), (n_col,), (n_col,), (n_col,), (n_col,), (n_row,), (n_row,),
        (n_row,), (n_row,), (n_col,), (n_col,),
    ]
    return pl.pallas_call(
        functools.partial(layer_kernel, n_col, n_row, inner, pieces),
        out_shape=(
            jax.ShapeDtypeStruct((rows_dev, width), BF16),
            jax.ShapeDtypeStruct((rows_dev, width), F32),
            jax.ShapeDtypeStruct((width, width), F32),
        ),
        in_specs=[smem] * 3 + [vmem] * 4,
        out_specs=(vmem, vmem, vmem),
        scratch_shapes=[pltpu.VMEM(shape, kind) for shape, kind in buffers] + [dma(s) for s in sems],
        compiler_params=pltpu.CompilerParams(
            collective_id=0, has_side_effects=True, vmem_limit_bytes=56 * 2**20
        ),
        name="layer",
    )(
        tile_rows.reshape(slots), tile_cols.reshape(slots), tile_count.reshape(1),
        features, weight, tiles[0, 0], cotangent,
    )


def solution(mesh):
    placed = (
        P(("row", "col"), None),
        P(),
        P("col", "row", None, None, None),
        P("col", "row", None),
        P("col", "row", None),
        P("col", "row"),
        P(("col", "row"), None),
    )
    return jax.shard_map(
        functools.partial(shards, mesh.shape["col"], mesh.shape["row"]),
        mesh=mesh,
        in_specs=placed,
        out_specs=(P(("col", "row"), None), P(("row", "col"), None), P()),
        check_vma=False,
    )
```

time: 302 us -> 67.1 us (0.22)
  waiting for transfers between devices: 249 us -> 0 us
  Pallas kernels: 0 us -> 61 us
  between operations: 14.6 us -> 1.3 us
  matrix products: 12 us -> 0 us
  blocking collectives: 8.66 us -> 0 us
  local copies, waits for them, and re-layouts: 13.1 us -> 4.58 us
    psum x1 -> x0, waiting for transfers between devices: 135 us -> none  [shards(): grad_w = lax.psum(weight_terms, ('col', 'row'))]
    reduce_scatter x2 -> x0, waiting for transfers between devices: 72.1 us -> none  [the longest x1 65 us: shards(): lax.psum_scatter(partial_value, 'row', scatter_dimension=0, tiled=True)]
    pallas_call x0 -> x1, Pallas kernels: none -> 61 us  [shards(): pl.pallas_call(functools.partial(layer_kernel, n_col, n_row, inner, piece...]
    all_gather x1 -> x0, waiting for transfers between devices: 41.5 us -> none  [shards(): gathered = lax.all_gather(cotangent, 'row', axis=0, tiled=True)]
    dot_general x7 -> x0, matrix products: 12 us -> none  [the longest x1 3.02 us: shards(): jnp.dot(features.T, grad_y, precision=lax.Precision.HIGHEST, preferred_el...]
    all_gather x1 -> x0, blocking collectives: 8.66 us -> none  [shards(): source = lax.all_gather(local_rows, 'col', axis=0, tiled=True)]
    dot_general x4 -> x0, local copies, waits for them, and re-layouts: 8.16 us -> none  [the longest x1 2.56 us: shards(): jnp.einsum('it,taf->iaf', select_dst, tile_terms, precision=lax.Precision...]
  transfers between devices with their start and end apart: 4 -> 0, of which waited for: 4 -> 0; matrix products, arithmetic and copies ran while one was open for 6% -> 0% of each run, Pallas kernels for 0% -> 0%
where the time goes in v1:
time: 67.1 us; the launch traced here: 66.9 us
  Pallas kernels  61 us (91%)
  local copies, waits for them, and re-layouts  4.58 us (7%)
  between operations  1.3 us (2%)
    pallas_call x1, Pallas kernels, shards(): pl.pallas_call(functools.partial(layer_kernel, n_col, n_row, inner, piece...  61 us
    unnamed x5, local copies, waits for them, and re-layouts  4.58 us

profile of v1, /device:TPU:1, one launch (start us, length us, event | category | flops | bytes accessed | tf_op | source)
XLA Modules:
  0.0 66.9 jit_solution(10704044890762437832)
XLA Ops:
  1.3 61.0 %layer.1 = (bf16[128,512]{1,0:T(8,128)(2,1)}, f32[128,512]{1,0:T(8,128)}, f32[512,512]{1,0:T(8,128)}) custom-call(s32[6]{0:T(128)} %bitcast.6, s32[6]{0:T(128)} %bitcast.7, s32[1]{0:T(128)} %bitcast.4.count_ref, f32[128,512]{1,0:T(8,128)} %feat_ref.1, f32[512,512]{1,0:T(8,128)} %w_ref.1, bf16[6,128,128]{2,1,0:T(8,128)(2,1)} %bitcast.5, bf16[128,512]{1,0:T(8,128)(2,1)} %cot_ref.1), custom_call_target="tpu_custom_call" | custom-call | tf_op jit(solution)/shard_map/layer/pallas_call | solution.py:348
  62.3 0.0 copy-start
  62.3 1.6 %copy.14 = bf16[128,512]{1,0:T(8,128)(2,1)} copy(bf16[128,512]{1,0:T(8,128)(2,1)} %get-tuple-element.6) | data formatting | bytes 262144
  63.9 0.0 copy-done
  63.9 0.7 %copy.15 = f32[128,512]{1,0:T(8,128)} copy(f32[128,512]{1,0:T(8,128)S(1)} %copy-done) | data formatting | bytes 524288
  64.6 2.3 %copy.16 = f32[512,512]{1,0:T(8,128)} copy(f32[512,512]{1,0:T(8,128)} %get-tuple-element.8) | data formatting | bytes 2097152
Async XLA Ops:
  62.3 1.6 %copy-start = (f32[128,512]{1,0:T(8,128)S(1)}, f32[128,512]{1,0:T(8,128)}, u32[]{:S(2)}) copy-start(f32[128,512]{1,0:T(8,128)} %get-tuple-element.7) | copy-start | bytes 786436

commit v2 on v1

--- a/solution.py
+++ b/solution.py
@@ -1,4 +1,5 @@
 import functools
+import math
 
 import jax
 import jax.numpy as jnp
@@ -25,13 +26,13 @@
 
 
 def layer_kernel(
-    n_col, n_row, inner, pieces,
+    n_col, n_row, inner, near, pieces,
     rows_ref, cols_ref, count_ref, feat_ref, w_ref, tiles_ref, cot_ref,
     agg_ref, gx_ref, gw_ref,
-    feat_all, cot_all, pad, pad_t, a_ref, at_ref, w_hi, w_lo, proj, part, part_send, y_in, z_in,
-    back, back_send, c_in, g_part, g1_in, g1_sum, g2_in, gw_all,
-    feat_s, feat_r, cotz_s, coty_s, cot_r, py_s, py_r, pz_s, pz_r, c_s, c_r,
-    g1_s, g1_r, g2_s, g2_r, g3_s, g3_r, g4_s, g4_r,
+    feat_all, feat_t, ax_t, cot_all, pad, pad_t, a_ref, at_ref, w_hi, w_lo, proj, part, part_send, y_in, z_in,
+    back, back_send, c_in, g_sum, g_part, g1_in, g1_sum, g2_in, gw_all,
+    feat_s, feat_r, up_s, down_s, coty_s, cot_r, py_s, py_r, pz_s, pz_r, c_s, c_r,
+    g1_s, g1_r, g2_s, g2_r, g3_s, g3_r, g4_s, g4_r, g5_s,
 ):
     outer = n_row // inner
     slots, tile = tiles_ref.shape[0], tiles_ref.shape[1]
@@ -89,8 +90,10 @@
     cot_all[row] = cot_ref[...]
     pl.semaphore_wait(barrier, n_col + n_row - 2)
 
-    def cot_out(d):
-        send(cot_ref, cot_all.at[row], cotz_s.at[d], cot_r.at[row], {"row": out_at(d + 1) * inner + in_id})
+    def chain(o, step, sems, d):
+        slot = o * inner + in_id
+        to = out_id + step
+        send(cot_all.at[slot], cot_all.at[slot], sems.at[d], cot_r.at[slot], {"row": to * inner + in_id})
 
     def cot_forward(o, d_out):
         def one(d):
@@ -99,7 +102,9 @@
                  {"row": out_id * inner + in_at(d + 1)})
         each(inner - 1, one)
 
-    each(outer - 1, cot_out)
+    if outer > 1:
+        pl.when(out_id < outer - 1)(lambda: chain(out_id, 1, up_s, 0))
+        pl.when(out_id > 0)(lambda: chain(out_id, -1, down_s, 0))
     cot_forward(out_id, 0)
 
     def feat_out(d):
@@ -139,27 +144,72 @@
         if not (isinstance(d, int) and d == 0):
             landed(feat_all.at[c], feat_r.at[c])
         block = feat_all[c]
-        proj[pl.ds(pl.multiple_of(c * rows_dev, rows_dev), rows_dev), :] = (
+        at = pl.multiple_of(c * rows_dev, rows_dev)
+        proj[pl.ds(at, rows_dev), :] = (
             matmul(block, w_hi[...]) + matmul(block, w_lo[...])
         ).astype(BF16)
+        feat_t[:, pl.ds(at, rows_dev)] = block.T
 
     project(0)
-    each(n_col - 1, lambda d: project(d + 1))
 
     def pass_on(d):
-        o = out_at(d + 1)
-        landed(cot_all.at[o * inner + in_id], cot_r.at[o * inner + in_id])
-        cot_forward(o, d + 1)
-
-    each(outer - 1, pass_on)
-
-    def forward(d):
-        o = out_at(d + 1)
-        span = inner * rows_dev
-        block = a_ref[pl.ds(pl.multiple_of(o * span, span), span), :]
-        result = matmul(block, proj[...]).reshape(inner, rows_dev, width)
+        def from_below():
+            o = out_id - d
+            landed(cot_all.at[o * inner + in_id], cot_r.at[o * inner + in_id])
+            pl.when(out_id < outer - 1)(lambda: chain(o, 1, up_s, d))
+            cot_forward(o, o + 1)
+
+        def from_above():
+            o = out_id + d
+            landed(cot_all.at[o * inner + in_id], cot_r.at[o * inner + in_id])
+            pl.when(out_id > 0)(lambda: chain(o, -1, down_s, d))
+            cot_forward(o, o + 1)
+
+        pl.when(out_id - d >= 0)(from_below)
+        pl.when(out_id + d < outer)(from_above)
+
+    span = inner * rows_dev
+
+    def forward(o):
+        at = o * span if isinstance(o, int) else pl.multiple_of(o * span, span)
+        result = matmul(a_ref[pl.ds(at, span), :], proj[...]).reshape(inner, rows_dev, width)
         part[o] = result
         part_send[o] = result.astype(BF16)
+
+    def weight_term(d):
+        def add(o):
+            def one(e):
+                slot = o * inner + in_at(e + 1)
+                landed(cot_all.at[slot], cot_r.at[slot])
+            each(inner - 1, one)
+            block = ax_t[:, pl.ds(pl.multiple_of(o * span, span), span)]
+            g_sum[...] += matmul(block, cot_all[pl.ds(o * inner, inner)].reshape(span, width))
+
+        if isinstance(d, int) and d == 0:
+            add(out_id)
+        else:
+            pl.when(out_id - d >= 0)(lambda: add(out_id - d))
+            pl.when(out_id + d < outer)(lambda: add(out_id + d))
+
+    each(n_col - 1, lambda d: project(d + 1))
+    if outer > 1:
+        pass_on(1)
+    ax_t[...] = matmul(feat_t[...], at_ref[...]).astype(BF16)
+    g_sum[...] = jnp.zeros_like(g_sum)
+    each(outer - 2, lambda d: pass_on(d + 2))
+    each(outer, forward)
+    weight_term(0)
+    each(outer - 1, lambda d: weight_term(d + 1))
+    g_part[...] = g_sum[...].astype(BF16).reshape(n_col, g_rows, width)
+
+    def g1_out(d):
+        c = col_at(d + 1)
+        send(g_part.at[c], g1_in.at[col], g1_s.at[d], g1_r.at[col], {"col": c})
+
+    each(n_col - 1, g1_out)
+
+    def inner_out(d):
+        o = out_at(d + 1)
 
         def one(e):
             target = in_at(e + 1)
@@ -167,60 +217,14 @@
                  {"row": out_id * inner + target})
         each(inner - 1, one)
 
-    each(outer, forward)
-
-    def backward(d):
-        o = out_at(d)
-        span = inner * rows_dev
-
-        def one(e):
-            slot = o * inner + in_at(e + 1)
-            landed(cot_all.at[slot], cot_r.at[slot])
-        each(inner - 1, one)
-        block = at_ref[:, pl.ds(pl.multiple_of(o * span, span), span)]
-        cots = cot_all[pl.ds(o * inner, inner)].reshape(span, width)
-        term = matmul(block, cots)
-        if isinstance(d, int) and d == 0:
-            back[...] = term
-        else:
-            back[...] += term
-
-    backward(0)
-    each(outer - 1, lambda d: backward(d + 1))
+    each(outer, inner_out)
+
+    back[...] = matmul(at_ref[...], cot_all[...].reshape(n_row * rows_dev, width))
     back_send[...] = back[...].astype(BF16).reshape(n_col, rows_dev, width)
-
-    g_part[...] = matmul(
-        feat_all[...].reshape(n_col * rows_dev, width),
-        back_send[...].reshape(n_col * rows_dev, width),
-        ((0,), (0,)),
-    ).astype(BF16).reshape(n_col, g_rows, width)
-
-    def g1_out(d):
-        c = col_at(d + 1)
-        send(g_part.at[c], g1_in.at[col], g1_s.at[d], g1_r.at[col], {"col": c})
 
     def c_out(d):
         c = col_at(d + 1)
         send(back_send.at[c], c_in.at[col], c_s.at[d], c_r.at[col], {"col": c})
-
-    each(n_col - 1, g1_out)
-    each(n_col - 1, c_out)
-
-    def inner_sum(o):
-        def one(e):
-            source = in_at(e + 1)
-            landed(y_in.at[o, source], py_r.at[o, source])
-            part[o, in_id] += y_in[o, source].astype(F32)
-        each(inner - 1, one)
-
-    def outer_out(d):
-        o = out_at(d + 1)
-        inner_sum(o)
-        part_send[o, in_id] = part[o, in_id].astype(BF16)
-        send(part_send.at[o, in_id], z_in.at[out_id], pz_s.at[d], pz_r.at[out_id], {"row": o * inner + in_id})
-
-    each(outer - 1, outer_out)
-    inner_sum(out_id)
 
     gw_part = g_part[col].astype(F32)
     def g1_add(d, total):
@@ -236,16 +240,23 @@
         reducer(r, lambda: send(g1_sum.at[r], g2_in.at[row], g2_s.at[d], g2_r.at[row], {"row": r}))
 
     each(n_row - 1, g2_out)
-
-    def c_add(d):
-        c = col_at(d + 1)
-        landed(c_in.at[c], c_r.at[c])
-    each(n_col - 1, c_add)
-    grad_y = back[pl.ds(pl.multiple_of(col * rows_dev, rows_dev), rows_dev), :]
-    for d in range(n_col - 1):
-        grad_y = grad_y + c_in[col_at(d + 1)].astype(F32)
-    grad_y = grad_y.astype(BF16)
-    gx_ref[...] = matmul(grad_y, w_hi[...], ((1,), (1,))) + matmul(grad_y, w_lo[...], ((1,), (1,)))
+    each(n_col - 1, c_out)
+
+    def inner_sum(o):
+        def one(e):
+            source = in_at(e + 1)
+            landed(y_in.at[o, source], py_r.at[o, source])
+            part[o, in_id] += y_in[o, source].astype(F32)
+        each(inner - 1, one)
+
+    def outer_out(d):
+        o = out_at(d + 1)
+        inner_sum(o)
+        part_send[o, in_id] = part[o, in_id].astype(BF16)
+        send(part_send.at[o, in_id], z_in.at[out_id], pz_s.at[d], pz_r.at[out_id], {"row": o * inner + in_id})
+
+    each(outer - 1, outer_out)
+    inner_sum(out_id)
 
     def g2_sum():
         def g2_wait(d):
@@ -264,6 +275,16 @@
 
     reducer(row, g2_sum)
 
+    def c_add(d):
+        c = col_at(d + 1)
+        landed(c_in.at[c], c_r.at[c])
+    each(n_col - 1, c_add)
+    grad_y = back[pl.ds(pl.multiple_of(col * rows_dev, rows_dev), rows_dev), :]
+    for d in range(n_col - 1):
+        grad_y = grad_y + c_in[col_at(d + 1)].astype(F32)
+    grad_y = grad_y.astype(BF16)
+    gx_ref[...] = matmul(grad_y, w_hi[...], ((1,), (1,))) + matmul(grad_y, w_lo[...], ((1,), (1,)))
+
     def z_wait(d):
         o = out_at(d + 1)
         landed(z_in.at[o], pz_r.at[o])
@@ -272,43 +293,94 @@
     each(outer - 1, z_wait)
     agg_ref[...] = part[out_id, in_id].astype(BF16)
 
+    def outer_col(d):
+        return lax.rem(col // near + d, n_col // near) * near + col % near
+
+    def near_col(d):
+        return col // near * near + lax.rem(col % near + d, near)
+
+    def to_near(c, r, d):
+        def one(e):
+            send(gw_all.at[c, r], gw_all.at[c, r], g5_s.at[d, r, e], g4_r.at[c, r], {"col": near_col(e + 1)})
+        each(near - 1, one)
+
+    def piece_out(r):
+        def one(d):
+            send(gw_all.at[col, r], gw_all.at[col, r], g4_s.at[d, r], g4_r.at[col, r], {"col": outer_col(d + 1)})
+        each(n_col // near - 1, one)
+        to_near(col, r, 0)
+
     def g3_wait(d):
         r = row_at(d + 1)
-        reducer(r, lambda: landed(gw_all.at[col, r], g3_r.at[r]))
-
+
+        def piece():
+            landed(gw_all.at[col, r], g3_r.at[r])
+            piece_out(r)
+        reducer(r, piece)
+
+    reducer(row, lambda: piece_out(row))
     each(n_row - 1, g3_wait)
 
-    def g4_out(d):
-        send(gw_all.at[col], gw_all.at[col], g4_s.at[d], g4_r.at[col], {"col": col_at(d + 1)})
-
-    each(n_col - 1, g4_out)
-
-    def g4_wait(d):
-        c = col_at(d + 1)
-        landed(gw_all.at[c], g4_r.at[c])
-        gw_ref[pl.ds(pl.multiple_of(c * g_rows, g_rows), g_rows), :] = (
-            gw_all[c].reshape(g_rows, width).astype(F32))
-
-    gw_ref[pl.ds(pl.multiple_of(col * g_rows, g_rows), g_rows), :] = (
-        gw_all[col].reshape(g_rows, width).astype(F32))
-    each(n_col - 1, g4_wait)
+    def pass_piece(d):
+        c = outer_col(d + 1)
+
+        def one(e):
+            r = row_at(e)
+
+            def piece():
+                landed(gw_all.at[c, r], g4_r.at[c, r])
+                to_near(c, r, d + 1)
+            reducer(r, piece)
+        each(n_row, one)
+
+    each(n_col // near - 1, pass_piece)
+
+    def last_wait(d):
+        def one(e):
+            c = near_col(e + 1)
+            c = lax.rem(c // near + d, n_col // near) * near + c % near
+            each(pieces, lambda r: landed(gw_all.at[c, r], g4_r.at[c, r]))
+        each(near - 1, one)
+
+    each(n_col // near, last_wait)
+    gw_ref[...] = gw_all[...].reshape(width, width)
 
     each(n_col - 1, lambda d: sent(feat_all.at[0], feat_s.at[d]))
-    each(outer - 1, lambda d: sent(cot_ref, cotz_s.at[d]))
-    each(outer, lambda d: each(inner - 1, lambda e: sent(cot_ref, coty_s.at[d, e])))
+    def chain_sent(d):
+        def up():
+            sent(cot_ref, up_s.at[d])
+
+        def down():
+            sent(cot_ref, down_s.at[d])
+        pl.when((out_id - d >= 0) & (out_id < outer - 1))(up)
+        pl.when((out_id + d < outer) & (out_id > 0))(down)
+
+    if outer > 1:
+        each(outer, chain_sent)
+    each(outer, lambda o: each(inner - 1, lambda e: sent(
+        cot_ref, coty_s.at[jnp.where(out_id == o, 0, o + 1), e])))
     each(outer, lambda d: each(inner - 1, lambda e: sent(y_in.at[0, 0], py_s.at[d, e])))
     each(outer - 1, lambda d: sent(z_in.at[0], pz_s.at[d]))
     each(n_col - 1, lambda d: sent(c_in.at[0], c_s.at[d]))
     each(n_col - 1, lambda d: sent(g1_in.at[0], g1_s.at[d]))
     each(n_row - 1, lambda d: reducer(row_at(d + 1), lambda: sent(g2_in.at[0], g2_s.at[d])))
     reducer(row, lambda: each(n_row - 1, lambda d: sent(g2_in.at[0], g3_s.at[d])))
-    each(n_col - 1, lambda d: sent(gw_all.at[0], g4_s.at[d]))
+    each(pieces, lambda r: each(n_col // near - 1, lambda d: sent(g2_in.at[0], g4_s.at[d, r])))
+    each(pieces, lambda r: each(n_col // near, lambda d: each(
+        near - 1, lambda e: sent(g2_in.at[0], g5_s.at[d, r, e]))))
+
+
+def write_kernel(agg_ref, gx_ref, gw_ref, agg_out, gx_out, gw_out):
+    agg_out[...] = agg_ref[...]
+    gx_out[...] = gx_ref[...]
+    gw_out[...] = gw_ref[...].astype(F32)
 
 
 def shards(n_col, n_row, features, weight, tiles, tile_rows, tile_cols, tile_count, cotangent):
     slots, tile = tiles.shape[2], tiles.shape[-1]
     rows_dev, width = features.shape
     inner = 2 if n_row % 2 == 0 else 1
+    near = 2 if n_col % 2 == 0 else 1
     outer = n_row // inner
     g_rows = width // n_col
     pieces = min(n_row, g_rows // 16)
@@ -319,6 +391,8 @@
     smem = pl.BlockSpec(memory_space=pltpu.SMEM)
     buffers = [
         ((n_col, rows_dev, width), BF16),
+        ((width, src), BF16),
+        ((width, dst), BF16),
         ((n_row, rows_dev, width), BF16),
         ((slots + 1, tile, tile), BF16),
         ((slots + 1, tile, tile), BF16),
@@ -334,35 +408,48 @@
         ((src, width), F32),
         ((n_col, rows_dev, width), BF16),
         ((n_col, rows_dev, width), BF16),
+        ((width, width), F32),
         ((n_col, g_rows, width), BF16),
         ((n_col, g_rows, width), BF16),
         ((pieces, g_piece, width), BF16),
         ((n_row, g_piece, width), BF16),
         ((n_col, pieces, g_piece, width), BF16),
     ]
+    limit = sum(math.prod(shape) * jnp.dtype(kind).itemsize for shape, kind in buffers) + 12 * 2**20
     sems = [
-        (n_col,), (n_col,), (outer,), (outer, inner), (n_row,), (outer, inner), (outer, inner),
+        (n_col,), (n_col,), (outer,), (outer,), (outer + 1, inner), (n_row,), (outer, inner), (outer, inner),
         (outer,), (outer,), (n_col,), (n_col,), (n_col,), (n_col,), (n_row,), (n_row,),
-        (n_row,), (n_row,), (n_col,), (n_col,),
+        (n_row,), (n_row,), (n_col, pieces), (n_col, pieces), (n_col, pieces, near),
     ]
-    return pl.pallas_call(
-        functools.partial(layer_kernel, n_col, n_row, inner, pieces),
+    aggregated, grad_x, grad_w = pl.pallas_call(
+        functools.partial(layer_kernel, n_col, n_row, inner, near, pieces),
         out_shape=(
             jax.ShapeDtypeStruct((rows_dev, width), BF16),
             jax.ShapeDtypeStruct((rows_dev, width), F32),
-            jax.ShapeDtypeStruct((width, width), F32),
+            jax.ShapeDtypeStruct((width, width), BF16),
         ),
         in_specs=[smem] * 3 + [vmem] * 4,
         out_specs=(vmem, vmem, vmem),
         scratch_shapes=[pltpu.VMEM(shape, kind) for shape, kind in buffers] + [dma(s) for s in sems],
         compiler_params=pltpu.CompilerParams(
-            collective_id=0, has_side_effects=True, vmem_limit_bytes=56 * 2**20
+            collective_id=0, has_side_effects=True, vmem_limit_bytes=limit
         ),
         name="layer",
     )(
         tile_rows.reshape(slots), tile_cols.reshape(slots), tile_count.reshape(1),
         features, weight, tiles[0, 0], cotangent,
     )
+    return pl.pallas_call(
+        write_kernel,
+        out_shape=(
+            jax.ShapeDtypeStruct((rows_dev, width), BF16),
+            jax.ShapeDtypeStruct((rows_dev, width), F32),
+            jax.ShapeDtypeStruct((width, width), F32),
+        ),
+        in_specs=[vmem] * 3,
+        out_specs=(vmem,) * 3,
+        name="write",
+    )(aggregated, grad_x, grad_w)
 
 
 def solution(mesh):

time: 67.1 us -> 65 us (0.969); the launches traced: 66.9 us -> 64 us
  Pallas kernels: 61 us -> 55.9 us
  local copies, waits for them, and re-layouts: 4.58 us -> 6.81 us
    pallas_call x1 -> x2, Pallas kernels: 61 us -> 55.9 us  [the longest x1 53.6 us: shards(): pl.pallas_call(functools.partial(layer_kernel, n_col, n_row, inner, near,...]
    unnamed x5 -> x18, local copies, waits for them, and re-layouts: 4.58 us -> 6.81 us
where the time goes in v2:
time: 65 us; the launch traced here: 64 us
  Pallas kernels  55.9 us (86%)
  local copies, waits for them, and re-layouts  6.81 us (10%)
  between operations  1.32 us (2%)
    pallas_call x1, Pallas kernels, shards(): pl.pallas_call(functools.partial(layer_kernel, n_col, n_row, inner, near,...  53.6 us
    unnamed x18, local copies, waits for them, and re-layouts  6.81 us
    pallas_call x1, Pallas kernels, shards(): pl.pallas_call(write_kernel, out_shape=(jax.ShapeDtypeStruct((rows_dev, w...  2.3 us

profile of v2, /device:TPU:1, one launch (start us, length us, event | category | flops | bytes accessed | tf_op | source)
XLA Modules:
  0.0 64.0 jit_solution(2220947333570992514)
XLA Ops:
  1.3 0.0 copy-start.7
  1.3 0.0 copy-start.8
  1.3 0.6 copy-done.7
  1.9 0.0 copy-done.8
  2.0 0.0 copy-start
  2.0 1.2 %copy-done = f32[512,512]{1,0:T(8,128)S(1)} copy-done((f32[512,512]{1,0:T(8,128)S(1)}, f32[512,512]{1,0:T(8,128)}, u32[]{:S(2)}) %copy-start) | copy-done | bytes 1048600
  3.2 0.0 copy-start.3
  3.2 0.9 %copy-done.3 = f32[128,512]{1,0:T(8,128)S(1)} copy-done((f32[128,512]{1,0:T(8,128)S(1)}, f32[128,512]{1,0:T(8,128)}, u32[]{:S(2)}) %copy-start.3) | copy-done | bytes 262168
  4.1 0.0 copy-start.4
  4.1 0.9 %copy-done.4 = bf16[1,1,6,128,128]{4,3,2,1,0:T(8,128)(2,1)S(1)} copy-done((bf16[1,1,6,128,128]{4,3,2,1,0:T(8,128)(2,1)S(1)}, bf16[1,1,6,128,128]{4,3,2,1,0:T(8,128)(2,1)}, u32[]{:S(2)}) %copy-start.4) | copy-done | bytes 196632
  5.1 0.0 copy-start.6
  5.1 0.9 %copy-done.6 = bf16[128,512]{1,0:T(8,128)(2,1)S(1)} copy-done((bf16[128,512]{1,0:T(8,128)(2,1)S(1)}, bf16[128,512]{1,0:T(8,128)(2,1)}, u32[]{:S(2)}) %copy-start.6) | copy-done | bytes 131096
  6.0 53.6 %layer.1 = (bf16[128,512]{1,0:T(8,128)(2,1)S(1)}, f32[128,512]{1,0:T(8,128)S(1)}, bf16[512,512]{1,0:T(8,128)(2,1)S(1)}) custom-call(s32[6]{0:T(128)S(1)} %bitcast.6, s32[6]{0:T(128)S(1)} %bitcast.7, s32[1]{0:T(128)} %bitcast.4.count_ref, f32[128,512]{1,0:T(8,128)S(1)} %copy-done.3, f32[512,512]{1,0:T(8,128)S(1)} %copy-done, ...), custom_call_target="tpu_custom_call" | custom-call | tf_op jit(solution)/shard_map/layer/pallas_call | solution.py:424
  59.5 0.0 copy-start.1
  59.5 0.8 %copy-done.1 = bf16[512,512]{1,0:T(8,128)(2,1)} copy-done((bf16[512,512]{1,0:T(8,128)(2,1)}, bf16[512,512]{1,0:T(8,128)(2,1)S(1)}, u32[]{:S(2)}) %copy-start.1) | copy-done | bytes 524312
  60.3 0.0 copy-start.2
  60.3 0.7 %copy-done.2 = f32[128,512]{1,0:T(8,128)} copy-done((f32[128,512]{1,0:T(8,128)}, f32[128,512]{1,0:T(8,128)S(1)}, u32[]{:S(2)}) %copy-start.2) | copy-done | bytes 262168
  61.0 0.0 copy-start.5
  61.0 0.6 %copy-done.5 = bf16[128,512]{1,0:T(8,128)(2,1)} copy-done((bf16[128,512]{1,0:T(8,128)(2,1)}, bf16[128,512]{1,0:T(8,128)(2,1)S(1)}, u32[]{:S(2)}) %copy-start.5) | copy-done | bytes 131096
  61.7 2.3 %write.1 = (bf16[128,512]{1,0:T(8,128)(2,1)}, f32[128,512]{1,0:T(8,128)}, f32[512,512]{1,0:T(8,128)}) custom-call(bf16[128,512]{1,0:T(8,128)(2,1)} %copy-done.5, f32[128,512]{1,0:T(8,128)} %copy-done.2, bf16[512,512]{1,0:T(8,128)(2,1)} %copy-done.1), custom_call_target="tpu_custom_call" | custom-call | tf_op jit(solution)/shard_map/write/pallas_call | solution.py:442
Async XLA Ops:
  1.3 0.7 %copy-start.7 = (s32[1,1,6]{2,1,0:T(1,128)S(1)}, s32[1,1,6]{2,1,0:T(1,128)}, u32[]{:S(2)}) copy-start(s32[1,1,6]{2,1,0:T(1,128)} %param.10) | copy-start | bytes 76
  1.3 0.7 %copy-start.8 = (s32[1,1,6]{2,1,0:T(1,128)S(1)}, s32[1,1,6]{2,1,0:T(1,128)}, u32[]{:S(2)}) copy-start(s32[1,1,6]{2,1,0:T(1,128)} %param.11) | copy-start | bytes 76
  2.0 1.2 %copy-start = (f32[512,512]{1,0:T(8,128)S(1)}, f32[512,512]{1,0:T(8,128)}, u32[]{:S(2)}) copy-start(f32[512,512]{1,0:T(8,128)} %w_ref.1) | copy-start | bytes 3145732
  3.2 0.9 %copy-start.3 = (f32[128,512]{1,0:T(8,128)S(1)}, f32[128,512]{1,0:T(8,128)}, u32[]{:S(2)}) copy-start(f32[128,512]{1,0:T(8,128)} %feat_ref.1) | copy-start | bytes 786436
  4.1 0.9 %copy-start.4 = (bf16[1,1,6,128,128]{4,3,2,1,0:T(8,128)(2,1)S(1)}, bf16[1,1,6,128,128]{4,3,2,1,0:T(8,128)(2,1)}, u32[]{:S(2)}) copy-start(bf16[1,1,6,128,128]{4,3,2,1,0:T(8,128)(2,1)} %param.9) | copy-start | bytes 589828
  5.1 0.9 %copy-start.6 = (bf16[128,512]{1,0:T(8,128)(2,1)S(1)}, bf16[128,512]{1,0:T(8,128)(2,1)}, u32[]{:S(2)}) copy-start(bf16[128,512]{1,0:T(8,128)(2,1)} %cot_ref.1) | copy-start | bytes 393220
  59.5 0.8 %copy-start.1 = (bf16[512,512]{1,0:T(8,128)(2,1)}, bf16[512,512]{1,0:T(8,128)(2,1)S(1)}, u32[]{:S(2)}) copy-start(bf16[512,512]{1,0:T(8,128)(2,1)S(1)} %get-tuple-element.8.gw_ref) | copy-start | bytes 1572868
  60.3 0.7 %copy-start.2 = (f32[128,512]{1,0:T(8,128)}, f32[128,512]{1,0:T(8,128)S(1)}, u32[]{:S(2)}) copy-start(f32[128,512]{1,0:T(8,128)S(1)} %get-tuple-element.7.gx_ref) | copy-start | bytes 786436
  61.0 0.7 %copy-start.5 = (bf16[128,512]{1,0:T(8,128)(2,1)}, bf16[128,512]{1,0:T(8,128)(2,1)S(1)}, u32[]{:S(2)}) copy-start(bf16[128,512]{1,0:T(8,128)(2,1)S(1)} %get-tuple-element.6.agg_ref) | copy-start | bytes 393220

commit v3 on v2

--- a/solution.py
+++ b/solution.py
@@ -27,11 +27,12 @@
 
 def layer_kernel(
     n_col, n_row, inner, near, pieces,
-    rows_ref, cols_ref, count_ref, feat_ref, w_ref, tiles_ref, cot_ref,
+    rows_in, cols_in, count_in, feat_in, w_in, tiles_in, cot_ref,
     agg_ref, gx_ref, gw_ref,
+    rows_ref, cols_ref, count_ref, feat_ref, w_ref, tiles_ref,
     feat_all, feat_t, ax_t, cot_all, pad, pad_t, a_ref, at_ref, w_hi, w_lo, proj, part, part_send, y_in, z_in,
     back, back_send, c_in, g_sum, g_part, g1_in, g1_sum, g2_in, gw_all,
-    feat_s, feat_r, up_s, down_s, coty_s, cot_r, py_s, py_r, pz_s, pz_r, c_s, c_r,
+    in_s, feat_s, feat_r, up_s, down_s, coty_s, cot_r, py_s, py_r, pz_s, pz_r, c_s, c_r,
     g1_s, g1_r, g2_s, g2_r, g3_s, g3_r, g4_s, g4_r, g5_s,
 ):
     outer = n_row // inner
@@ -86,8 +87,18 @@
         barrier, inc=1, device_id={"col": col_at(d + 1)}, device_id_type=MESH))
     each(n_row - 1, lambda d: pl.semaphore_signal(
         barrier, inc=1, device_id={"row": row_at(d + 1)}, device_id_type=MESH))
+    fetches = [
+        pltpu.make_async_copy(source, target, in_s.at[k])
+        for k, (source, target) in enumerate((
+            (cot_ref, cot_all.at[row]), (feat_in, feat_ref), (tiles_in, tiles_ref),
+            (rows_in, rows_ref), (cols_in, cols_ref), (count_in, count_ref), (w_in, w_ref),
+        ))
+    ]
+    for fetch in fetches:
+        fetch.start()
+    fetches[1].wait()
     feat_all[col] = feat_ref[...].astype(BF16)
-    cot_all[row] = cot_ref[...]
+    fetches[0].wait()
     pl.semaphore_wait(barrier, n_col + n_row - 2)
 
     def chain(o, step, sems, d):
@@ -117,12 +128,14 @@
         pad[t] = one
         pad_t[t] = one.T
 
+    for fetch in fetches[2:]:
+        fetch.wait()
     each(slots, pad_one)
     pad[slots] = jnp.zeros((tile, tile), BF16)
     pad_t[slots] = jnp.zeros((tile, tile), BF16)
-    live = count_ref[0]
+    live = count_ref[0, 0]
     places = [
-        jnp.where(t < live, rows_ref[t] * src_tiles + cols_ref[t], -1) for t in range(slots)
+        jnp.where(t < live, rows_ref[0, 0, t] * src_tiles + cols_ref[0, 0, t], -1) for t in range(slots)
     ]
 
     def lay(i):
@@ -191,23 +204,6 @@
             pl.when(out_id - d >= 0)(lambda: add(out_id - d))
             pl.when(out_id + d < outer)(lambda: add(out_id + d))
 
-    each(n_col - 1, lambda d: project(d + 1))
-    if outer > 1:
-        pass_on(1)
-    ax_t[...] = matmul(feat_t[...], at_ref[...]).astype(BF16)
-    g_sum[...] = jnp.zeros_like(g_sum)
-    each(outer - 2, lambda d: pass_on(d + 2))
-    each(outer, forward)
-    weight_term(0)
-    each(outer - 1, lambda d: weight_term(d + 1))
-    g_part[...] = g_sum[...].astype(BF16).reshape(n_col, g_rows, width)
-
-    def g1_out(d):
-        c = col_at(d + 1)
-        send(g_part.at[c], g1_in.at[col], g1_s.at[d], g1_r.at[col], {"col": c})
-
-    each(n_col - 1, g1_out)
-
     def inner_out(d):
         o = out_at(d + 1)
 
@@ -217,7 +213,26 @@
                  {"row": out_id * inner + target})
         each(inner - 1, one)
 
-    each(outer, inner_out)
+    if outer > 1:
+        pass_on(1)
+    each(n_col - 1, lambda d: project(d + 1))
+    each(min(outer - 2, 1), lambda d: pass_on(2))
+    each(outer, forward)
+    each(outer - 3, lambda d: pass_on(d + 3))
+    first = outer // 2
+    each(first, inner_out)
+    ax_t[...] = matmul(feat_t[...], at_ref[...]).astype(BF16)
+    g_sum[...] = jnp.zeros_like(g_sum)
+    weight_term(0)
+    each(outer - 1, lambda d: weight_term(d + 1))
+    g_part[...] = g_sum[...].astype(BF16).reshape(n_col, g_rows, width)
+
+    def g1_out(d):
+        c = col_at(d + 1)
+        send(g_part.at[c], g1_in.at[col], g1_s.at[d], g1_r.at[col], {"col": c})
+
+    each(n_col - 1, g1_out)
+    each(outer - first, lambda d: inner_out(d + first))
 
     back[...] = matmul(at_ref[...], cot_all[...].reshape(n_row * rows_dev, width))
     back_send[...] = back[...].astype(BF16).reshape(n_col, rows_dev, width)
@@ -225,6 +240,21 @@
     def c_out(d):
         c = col_at(d + 1)
         send(back_send.at[c], c_in.at[col], c_s.at[d], c_r.at[col], {"col": c})
+
+    def inner_sum(o):
+        def one(e):
+            source = in_at(e + 1)
+            landed(y_in.at[o, source], py_r.at[o, source])
+            part[o, in_id] += y_in[o, source].astype(F32)
+        each(inner - 1, one)
+
+    def outer_out(d):
+        o = out_at(d + 1)
+        inner_sum(o)
+        part_send[o, in_id] = part[o, in_id].astype(BF16)
+        send(part_send.at[o, in_id], z_in.at[out_id], pz_s.at[d], pz_r.at[out_id], {"row": o * inner + in_id})
+
+    each(outer - 1, outer_out)
 
     gw_part = g_part[col].astype(F32)
     def g1_add(d, total):
@@ -242,20 +272,6 @@
     each(n_row - 1, g2_out)
     each(n_col - 1, c_out)
 
-    def inner_sum(o):
-        def one(e):
-            source = in_at(e + 1)
-            landed(y_in.at[o, source], py_r.at[o, source])
-            part[o, in_id] += y_in[o, source].astype(F32)
-        each(inner - 1, one)
-
-    def outer_out(d):
-        o = out_at(d + 1)
-        inner_sum(o)
-        part_send[o, in_id] = part[o, in_id].astype(BF16)
-        send(part_send.at[o, in_id], z_in.at[out_id], pz_s.at[d], pz_r.at[out_id], {"row": o * inner + in_id})
-
-    each(outer - 1, outer_out)
     inner_sum(out_id)
 
     def g2_sum():
@@ -275,6 +291,42 @@
 
     reducer(row, g2_sum)
 
+    def z_wait(d):
+        o = out_at(d + 1)
+        landed(z_in.at[o], pz_r.at[o])
+        part[out_id, in_id] += z_in[o].astype(F32)
+
+    each(outer - 1, z_wait)
+    agg_ref[...] = part[out_id, in_id].astype(BF16)
+
+    def outer_col(d):
+        return lax.rem(col // near + d, n_col // near) * near + col % near
+
+    def near_col(d):
+        return col // near * near + lax.rem(col % near + d, near)
+
+    def to_near(c, r, d):
+        def one(e):
+            send(gw_all.at[c, r], gw_all.at[c, r], g5_s.at[d, r, e], g4_r.at[c, r], {"col": near_col(e + 1)})
+        each(near - 1, one)
+
+    def piece_out(r):
+        def one(d):
+            send(gw_all.at[col, r], gw_all.at[col, r], g4_s.at[d, r], g4_r.at[col, r], {"col": outer_col(d + 1)})
+        each(n_col // near - 1, one)
+        to_near(col, r, 0)
+
+    def g3_wait(d):
+        r = row_at(d + 1)
+
+        def piece():
+            landed(gw_all.at[col, r], g3_r.at[r])
+            piece_out(r)
+        reducer(r, piece)
+
+    reducer(row, lambda: piece_out(row))
+    each(n_row - 1, g3_wait)
+
     def c_add(d):
         c = col_at(d + 1)
         landed(c_in.at[c], c_r.at[c])
@@ -284,42 +336,6 @@
         grad_y = grad_y + c_in[col_at(d + 1)].astype(F32)
     grad_y = grad_y.astype(BF16)
     gx_ref[...] = matmul(grad_y, w_hi[...], ((1,), (1,))) + matmul(grad_y, w_lo[...], ((1,), (1,)))
-
-    def z_wait(d):
-        o = out_at(d + 1)
-        landed(z_in.at[o], pz_r.at[o])
-        part[out_id, in_id] += z_in[o].astype(F32)
-
-    each(outer - 1, z_wait)
-    agg_ref[...] = part[out_id, in_id].astype(BF16)
-
-    def outer_col(d):
-        return lax.rem(col // near + d, n_col // near) * near + col % near
-
-    def near_col(d):
-        return col // near * near + lax.rem(col % near + d, near)
-
-    def to_near(c, r, d):
-        def one(e):
-            send(gw_all.at[c, r], gw_all.at[c, r], g5_s.at[d, r, e], g4_r.at[c, r], {"col": near_col(e + 1)})
-        each(near - 1, one)
-
-    def piece_out(r):
-        def one(d):
-            send(gw_all.at[col, r], gw_all.at[col, r], g4_s.at[d, r], g4_r.at[col, r], {"col": outer_col(d + 1)})
-        each(n_col // near - 1, one)
-        to_near(col, r, 0)
-
-    def g3_wait(d):
-        r = row_at(d + 1)
-
-        def piece():
-            landed(gw_all.at[col, r], g3_r.at[r])
-            piece_out(r)
-        reducer(r, piece)
-
-    reducer(row, lambda: piece_out(row))
-    each(n_row - 1, g3_wait)
 
     def pass_piece(d):
         c = outer_col(d + 1)
@@ -370,10 +386,21 @@
         near - 1, lambda e: sent(g2_in.at[0], g5_s.at[d, r, e]))))
 
 
-def write_kernel(agg_ref, gx_ref, gw_ref, agg_out, gx_out, gw_out):
-    agg_out[...] = agg_ref[...]
-    gx_out[...] = gx_ref[...]
-    gw_out[...] = gw_ref[...].astype(F32)
+def write_kernel(agg_ref, gx_ref, gw_ref, agg_out, gx_out, gw_out, narrow, wide, sems):
+    copies = [
+        pltpu.make_async_copy(agg_ref, agg_out, sems.at[0]),
+        pltpu.make_async_copy(gx_ref, gx_out, sems.at[1]),
+    ]
+    load = pltpu.make_async_copy(gw_ref, narrow, sems.at[2])
+    load.start()
+    for copy in copies:
+        copy.start()
+    load.wait()
+    wide[...] = narrow[...].astype(F32)
+    store = pltpu.make_async_copy(wide, gw_out, sems.at[3])
+    store.start()
+    for copy in copies + [store]:
+        copy.wait()
 
 
 def shards(n_col, n_row, features, weight, tiles, tile_rows, tile_cols, tile_count, cotangent):
@@ -388,8 +415,12 @@
     src, dst = n_col * rows_dev, n_row * rows_dev
     dma = pltpu.SemaphoreType.DMA
     vmem = pl.BlockSpec(memory_space=pltpu.VMEM)
-    smem = pl.BlockSpec(memory_space=pltpu.SMEM)
+    hbm = pl.BlockSpec(memory_space=pltpu.HBM)
+    anywhere = pl.BlockSpec(memory_space=pl.ANY)
     buffers = [
+        (features.shape, F32),
+        (weight.shape, F32),
+        (tiles.shape[2:], BF16),
         ((n_col, rows_dev, width), BF16),
         ((width, src), BF16),
         ((width, dst), BF16),
@@ -415,9 +446,10 @@
         ((n_row, g_piece, width), BF16),
         ((n_col, pieces, g_piece, width), BF16),
     ]
-    limit = sum(math.prod(shape) * jnp.dtype(kind).itemsize for shape, kind in buffers) + 12 * 2**20
+    held = sum(math.prod(shape) * jnp.dtype(kind).itemsize for shape, kind in buffers)
+    limit = max(56 * 2**20, min(held + 12 * 2**20, 63 * 2**20))
     sems = [
-        (n_col,), (n_col,), (outer,), (outer,), (outer + 1, inner), (n_row,), (outer, inner), (outer, inner),
+        (7,), (n_col,), (n_col,), (outer,), (outer,), (outer + 1, inner), (n_row,), (outer, inner), (outer, inner),
         (outer,), (outer,), (n_col,), (n_col,), (n_col,), (n_col,), (n_row,), (n_row,),
         (n_row,), (n_row,), (n_col, pieces), (n_col, pieces), (n_col, pieces, near),
     ]
@@ -428,15 +460,16 @@
             jax.ShapeDtypeStruct((rows_dev, width), F32),
             jax.ShapeDtypeStruct((width, width), BF16),
         ),
-        in_specs=[smem] * 3 + [vmem] * 4,
+        in_specs=[hbm] * 7,
         out_specs=(vmem, vmem, vmem),
-        scratch_shapes=[pltpu.VMEM(shape, kind) for shape, kind in buffers] + [dma(s) for s in sems],
+        scratch_shapes=[pltpu.SMEM(one.shape, jnp.int32) for one in (tile_rows, tile_cols, tile_count)]
+        + [pltpu.VMEM(shape, kind) for shape, kind in buffers] + [dma(s) for s in sems],
         compiler_params=pltpu.CompilerParams(
             collective_id=0, has_side_effects=True, vmem_limit_bytes=limit
         ),
         name="layer",
     )(
-        tile_rows.reshape(slots), tile_cols.reshape(slots), tile_count.reshape(1),
+        tile_rows, tile_cols, tile_count,
         features, weight, tiles[0, 0], cotangent,
     )
     return pl.pallas_call(
@@ -446,8 +479,12 @@
             jax.ShapeDtypeStruct((rows_dev, width), F32),
             jax.ShapeDtypeStruct((width, width), F32),
         ),
-        in_specs=[vmem] * 3,
-        out_specs=(vmem,) * 3,
+        in_specs=[anywhere] * 3,
+        out_specs=(hbm,) * 3,
+        scratch_shapes=[
+            pltpu.VMEM((width, width), BF16), pltpu.VMEM((width, width), F32), dma((4,)),
+        ],
+        compiler_params=pltpu.CompilerParams(vmem_limit_bytes=limit),
         name="write",
     )(aggregated, grad_x, grad_w)
 

time: 65 us -> 65.4 us (level); the launches traced: 64 us -> 65.2 us
  Pallas kernels: 55.9 us -> 63.9 us
  local copies, waits for them, and re-layouts: 6.81 us -> 0 us
    pallas_call x1, Pallas kernels: 2.3 us -> 13.1 us  [shards(): pl.pallas_call(write_kernel, out_shape=(jax.ShapeDtypeStruct((rows_dev, w...]
    unnamed x18 -> x0, local copies, waits for them, and re-layouts: 6.81 us -> none
    pallas_call x1, Pallas kernels: 53.6 us -> 50.9 us  [shards(): pl.pallas_call(functools.partial(layer_kernel, n_col, n_row, inner, near,...]
where the time goes in v3:
time: 65.4 us; the launch traced here: 65.2 us
  Pallas kernels  63.9 us (98%)
  between operations  1.29 us (2%)
    pallas_call x1, Pallas kernels, shards(): pl.pallas_call(functools.partial(layer_kernel, n_col, n_row, inner, near,...  50.9 us
    pallas_call x1, Pallas kernels, shards(): pl.pallas_call(write_kernel, out_shape=(jax.ShapeDtypeStruct((rows_dev, w...  13.1 us

profile of v3, /device:TPU:1, one launch (start us, length us, event | category | flops | bytes accessed | tf_op | source)
XLA Modules:
  0.0 65.2 jit_solution(15296331132181233673)
XLA Ops:
  1.3 50.9 %layer.1 = (bf16[128,512]{1,0:T(8,128)(2,1)}, f32[128,512]{1,0:T(8,128)}, bf16[512,512]{1,0:T(8,128)(2,1)}) custom-call(s32[1,1,6]{2,1,0:T(1,128)} %rows_in.1, s32[1,1,6]{2,1,0:T(1,128)} %cols_in.1, s32[1,1]{1,0:T(1,128)S(6)} %copy.10.count_in, f32[128,512]{1,0:T(8,128)} %feat_in.1, f32[512,512]{1,0:T(8,128)} %w_in.1, bf16[6,128,128]{2,1,0:T(8,128)(2,1)} %bitcast.1, ...), custom_call_target="tpu_custom_call" | custom-call | tf_op jit(solution)/shard_map/layer/pallas_call | solution.py:456
  52.1 13.1 %write.1 = (bf16[128,512]{1,0:T(8,128)(2,1)}, f32[128,512]{1,0:T(8,128)}, f32[512,512]{1,0:T(8,128)}) custom-call(bf16[128,512]{1,0:T(8,128)(2,1)} %get-tuple-element.6.agg_ref, f32[128,512]{1,0:T(8,128)} %get-tuple-element.7.gx_ref, bf16[512,512]{1,0:T(8,128)(2,1)} %get-tuple-element.8.gw_ref), custom_call_target="tpu_custom_call" | custom-call | tf_op jit(solution)/shard_map/write/pallas_call | solution.py:475

commit v4 on v3

--- a/solution.py
+++ b/solution.py
@@ -189,8 +189,10 @@
         part[o] = result
         part_send[o] = result.astype(BF16)
 
-    def weight_term(d):
-        def add(o):
+    def weight_term(k, _):
+        o = out_id + jnp.where(k % 2 == 1, -((k + 1) // 2), k // 2)
+
+        def add():
             def one(e):
                 slot = o * inner + in_at(e + 1)
                 landed(cot_all.at[slot], cot_r.at[slot])
@@ -198,11 +200,7 @@
             block = ax_t[:, pl.ds(pl.multiple_of(o * span, span), span)]
             g_sum[...] += matmul(block, cot_all[pl.ds(o * inner, inner)].reshape(span, width))
 
-        if isinstance(d, int) and d == 0:
-            add(out_id)
-        else:
-            pl.when(out_id - d >= 0)(lambda: add(out_id - d))
-            pl.when(out_id + d < outer)(lambda: add(out_id + d))
+        pl.when((o >= 0) & (o < outer))(add)
 
     def inner_out(d):
         o = out_at(d + 1)
@@ -217,14 +215,13 @@
         pass_on(1)
     each(n_col - 1, lambda d: project(d + 1))
     each(min(outer - 2, 1), lambda d: pass_on(2))
-    each(outer, forward)
+    lax.fori_loop(0, outer, lambda o, _: forward(o), None)
     each(outer - 3, lambda d: pass_on(d + 3))
     first = outer // 2
     each(first, inner_out)
     ax_t[...] = matmul(feat_t[...], at_ref[...]).astype(BF16)
     g_sum[...] = jnp.zeros_like(g_sum)
-    weight_term(0)
-    each(outer - 1, lambda d: weight_term(d + 1))
+    lax.fori_loop(0, 2 * outer - 1, weight_term, None)
     g_part[...] = g_sum[...].astype(BF16).reshape(n_col, g_rows, width)
 
     def g1_out(d):
@@ -386,21 +383,26 @@
         near - 1, lambda e: sent(g2_in.at[0], g5_s.at[d, r, e]))))
 
 
-def write_kernel(agg_ref, gx_ref, gw_ref, agg_out, gx_out, gw_out, narrow, wide, sems):
-    copies = [
-        pltpu.make_async_copy(agg_ref, agg_out, sems.at[0]),
-        pltpu.make_async_copy(gx_ref, gx_out, sems.at[1]),
+def write_kernel(agg_ref, gx_ref, gw_ref, agg_out, gx_out, gw_out, agg, gx, narrow, wide, sems):
+    loads = [
+        pltpu.make_async_copy(source, target, sems.at[k])
+        for k, (source, target) in enumerate(((gw_ref, narrow), (agg_ref, agg), (gx_ref, gx)))
     ]
-    load = pltpu.make_async_copy(gw_ref, narrow, sems.at[2])
-    load.start()
-    for copy in copies:
-        copy.start()
-    load.wait()
+    stores = [
+        pltpu.make_async_copy(source, target, sems.at[3 + k])
+        for k, (source, target) in enumerate(((wide, gw_out), (agg, agg_out), (gx, gx_out)))
+    ]
+    for load in loads:
+        load.start()
+    for k in (1, 2):
+        loads[k].wait()
+        stores[k].start()
+    loads[0].wait()
     wide[...] = narrow[...].astype(F32)
-    store = pltpu.make_async_copy(wide, gw_out, sems.at[3])
-    store.start()
-    for copy in copies + [store]:
-        copy.wait()
+    for k in (0, 1, 2):
+        if k == 0:
+            stores[k].start()
+        stores[k].wait()
 
 
 def shards(n_col, n_row, features, weight, tiles, tile_rows, tile_cols, tile_count, cotangent):
@@ -482,7 +484,8 @@
         in_specs=[anywhere] * 3,
         out_specs=(hbm,) * 3,
         scratch_shapes=[
-            pltpu.VMEM((width, width), BF16), pltpu.VMEM((width, width), F32), dma((4,)),
+            pltpu.VMEM((rows_dev, width), BF16), pltpu.VMEM((rows_dev, width), F32),
+            pltpu.VMEM((width, width), BF16), pltpu.VMEM((width, width), F32), dma((6,)),
         ],
         compiler_params=pltpu.CompilerParams(vmem_limit_bytes=limit),
         name="write",

time: 65.4 us -> 54.6 us (0.83)
  Pallas kernels: 63.9 us -> 53.1 us
    pallas_call x1, Pallas kernels: 13.1 us -> 2.26 us  [shards(): pl.pallas_call(write_kernel, out_shape=(jax.ShapeDtypeStruct((rows_dev, w...]
where the time goes in v4:
time: 54.6 us; the launch traced here: 54.4 us
  Pallas kernels  53.1 us (97%)
  between operations  1.29 us (2%)
    pallas_call x1, Pallas kernels, shards(): pl.pallas_call(functools.partial(layer_kernel, n_col, n_row, inner, near,...  50.9 us
    pallas_call x1, Pallas kernels, shards(): pl.pallas_call(write_kernel, out_shape=(jax.ShapeDtypeStruct((rows_dev, w...  2.26 us

profile of v4, /device:TPU:1, one launch (start us, length us, event | category | flops | bytes accessed | tf_op | source)
XLA Modules:
  0.0 54.4 jit_solution(2304078483746341930)
XLA Ops:
  1.3 50.9 %layer.1 = (bf16[128,512]{1,0:T(8,128)(2,1)}, f32[128,512]{1,0:T(8,128)}, bf16[512,512]{1,0:T(8,128)(2,1)}) custom-call(s32[1,1,6]{2,1,0:T(1,128)} %rows_in.1, s32[1,1,6]{2,1,0:T(1,128)} %cols_in.1, s32[1,1]{1,0:T(1,128)S(6)} %copy.10.count_in, f32[128,512]{1,0:T(8,128)} %feat_in.1, f32[512,512]{1,0:T(8,128)} %w_in.1, bf16[6,128,128]{2,1,0:T(8,128)(2,1)} %bitcast.1, ...), custom_call_target="tpu_custom_call" | custom-call | tf_op jit(solution)/shard_map/layer/pallas_call | solution.py:458
  52.2 2.3 %write.1 = (bf16[128,512]{1,0:T(8,128)(2,1)}, f32[128,512]{1,0:T(8,128)}, f32[512,512]{1,0:T(8,128)}) custom-call(bf16[128,512]{1,0:T(8,128)(2,1)} %get-tuple-element.6.agg_ref, f32[128,512]{1,0:T(8,128)} %get-tuple-element.7.gx_ref, bf16[512,512]{1,0:T(8,128)(2,1)} %get-tuple-element.8.gw_ref), custom_call_target="tpu_custom_call" | custom-call | tf_op jit(solution)/shard_map/write/pallas_call | solution.py:477

commit v5 on v4

--- a/solution.py
+++ b/solution.py
@@ -123,6 +123,22 @@
 
     each(n_col - 1, feat_out)
 
+    def pass_on(d):
+        def from_below():
+            o = out_id - d
+            landed(cot_all.at[o * inner + in_id], cot_r.at[o * inner + in_id])
+            pl.when(out_id < outer - 1)(lambda: chain(o, 1, up_s, d))
+            cot_forward(o, o + 1)
+
+        def from_above():
+            o = out_id + d
+            landed(cot_all.at[o * inner + in_id], cot_r.at[o * inner + in_id])
+            pl.when(out_id > 0)(lambda: chain(o, -1, down_s, d))
+            cot_forward(o, o + 1)
+
+        pl.when(out_id - d >= 0)(from_below)
+        pl.when(out_id + d < outer)(from_above)
+
     def pad_one(t):
         one = tiles_ref[t]
         pad[t] = one
@@ -147,7 +163,11 @@
             a_ref[pl.ds(at, tile), k * tile:(k + 1) * tile] = pad[index]
             at_ref[k * tile:(k + 1) * tile, pl.ds(at, tile)] = pad_t[index]
 
-    each(dst_tiles, lay)
+    half = dst_tiles // 2
+    each(half, lay)
+    if outer > 1:
+        pass_on(1)
+    each(dst_tiles - half, lambda i: lay(i + half))
     weight = w_ref[...]
     w_hi[...] = weight.astype(BF16)
     w_lo[...] = (weight - w_hi[...].astype(F32)).astype(BF16)
@@ -165,22 +185,6 @@
 
     project(0)
 
-    def pass_on(d):
-        def from_below():
-            o = out_id - d
-            landed(cot_all.at[o * inner + in_id], cot_r.at[o * inner + in_id])
-            pl.when(out_id < outer - 1)(lambda: chain(o, 1, up_s, d))
-            cot_forward(o, o + 1)
-
-        def from_above():
-            o = out_id + d
-            landed(cot_all.at[o * inner + in_id], cot_r.at[o * inner + in_id])
-            pl.when(out_id > 0)(lambda: chain(o, -1, down_s, d))
-            cot_forward(o, o + 1)
-
-        pl.when(out_id - d >= 0)(from_below)
-        pl.when(out_id + d < outer)(from_above)
-
     span = inner * rows_dev
 
     def forward(o):
@@ -211,8 +215,6 @@
                  {"row": out_id * inner + target})
         each(inner - 1, one)
 
-    if outer > 1:
-        pass_on(1)
     each(n_col - 1, lambda d: project(d + 1))
     each(min(outer - 2, 1), lambda d: pass_on(2))
     lax.fori_loop(0, outer, lambda o, _: forward(o), None)
@@ -251,7 +253,8 @@
         part_send[o, in_id] = part[o, in_id].astype(BF16)
         send(part_send.at[o, in_id], z_in.at[out_id], pz_s.at[d], pz_r.at[out_id], {"row": o * inner + in_id})
 
-    each(outer - 1, outer_out)
+    early = max(outer - 2, 0)
+    each(min(early, 1), outer_out)
 
     gw_part = g_part[col].astype(F32)
     def g1_add(d, total):
@@ -269,6 +272,8 @@
     each(n_row - 1, g2_out)
     each(n_col - 1, c_out)
 
+    rest = outer - 1 - min(early, 1)
+    each(rest, lambda d: outer_out(d + outer - 1 - rest))
     inner_sum(out_id)
 
     def g2_sum():
@@ -288,14 +293,6 @@
 
     reducer(row, g2_sum)
 
-    def z_wait(d):
-        o = out_at(d + 1)
-        landed(z_in.at[o], pz_r.at[o])
-        part[out_id, in_id] += z_in[o].astype(F32)
-
-    each(outer - 1, z_wait)
-    agg_ref[...] = part[out_id, in_id].astype(BF16)
-
     def outer_col(d):
         return lax.rem(col // near + d, n_col // near) * near + col % near
 
@@ -347,6 +344,14 @@
         each(n_row, one)
 
     each(n_col // near - 1, pass_piece)
+
+    def z_wait(d):
+        o = out_at(d + 1)
+        landed(z_in.at[o], pz_r.at[o])
+        part[out_id, in_id] += z_in[o].astype(F32)
+
+    each(outer - 1, z_wait)
+    agg_ref[...] = part[out_id, in_id].astype(BF16)
 
     def last_wait(d):
         def one(e):

time: 54.6 us -> 54.3 us (level)
  no operation moved by 1% of the time
where the time goes in v5:
time: 54.3 us; the launch traced here: 54.1 us
  Pallas kernels  52.8 us (97%)
  between operations  1.29 us (2%)
    pallas_call x1, Pallas kernels, shards(): pl.pallas_call(functools.partial(layer_kernel, n_col, n_row, inner, near,...  50.5 us
    pallas_call x1, Pallas kernels, shards(): pl.pallas_call(write_kernel, out_shape=(jax.ShapeDtypeStruct((rows_dev, w...  2.26 us

profile of v5, /device:TPU:1, one launch (start us, length us, event | category | flops | bytes accessed | tf_op | source)
XLA Modules:
  0.0 54.1 jit_solution(4828578887563226974)
XLA Ops:
  1.3 50.5 %layer.1 = (bf16[128,512]{1,0:T(8,128)(2,1)}, f32[128,512]{1,0:T(8,128)}, bf16[512,512]{1,0:T(8,128)(2,1)}) custom-call(s32[1,1,6]{2,1,0:T(1,128)} %rows_in.1, s32[1,1,6]{2,1,0:T(1,128)} %cols_in.1, s32[1,1]{1,0:T(1,128)S(6)} %copy.10.count_in, f32[128,512]{1,0:T(8,128)} %feat_in.1, f32[512,512]{1,0:T(8,128)} %w_in.1, bf16[6,128,128]{2,1,0:T(8,128)(2,1)} %bitcast.1, ...), custom_call_target="tpu_custom_call" | custom-call | tf_op jit(solution)/shard_map/layer/pallas_call | solution.py:463
  51.8 2.3 %write.1 = (bf16[128,512]{1,0:T(8,128)(2,1)}, f32[128,512]{1,0:T(8,128)}, f32[512,512]{1,0:T(8,128)}) custom-call(bf16[128,512]{1,0:T(8,128)(2,1)} %get-tuple-element.6.agg_ref, f32[128,512]{1,0:T(8,128)} %get-tuple-element.7.gx_ref, bf16[512,512]{1,0:T(8,128)(2,1)} %get-tuple-element.8.gw_ref), custom_call_target="tpu_custom_call" | custom-call | tf_op jit(solution)/shard_map/write/pallas_call | solution.py:482

commit v6 on v4

v6 whole, which is shorter than its diff:
```python
import functools
import math

import jax
import jax.numpy as jnp
from jax import lax
from jax.experimental import pallas as pl
from jax.experimental.pallas import tpu as pltpu
from jax.sharding import PartitionSpec as P

BF16 = jnp.bfloat16
F32 = jnp.float32
MESH = pl.DeviceIdType.MESH


def each(count, body):
    if count <= 8:
        for step in range(count):
            body(step)
    else:
        lax.fori_loop(0, count, lambda step, _: (body(step), None)[1], None)


def matmul(a, b, contract=((1,), (0,))):
    return lax.dot_general(a, b, (contract, ((), ())), preferred_element_type=F32)


def layer_kernel(
    n_col, n_row, inner, near, pieces,
    rows_in, cols_in, count_in, feat_in, w_in, tiles_in, cot_ref,
    agg_ref, gx_ref, gw_ref,
    rows_ref, cols_ref, count_ref, rows_v, cols_v, count_v, feat_ref, w_ref, tiles_all,
    feat_all, feat_t, ax_t, cot_all, pad, pad_t, a_ref, at_ref, w_hi, w_lo, proj, part, part_send, z_in,
    back, back_send, n1_in, n1_sum, n2_in, n2_sum, n3_in, g_sum, g_part, g1_in, g1_sum, g2_in, gw_all,
    in_s, move_s, y_s, y_r, fx_s, fn_s, ff_s, feat_r, up_s, down_s, cot_r, pz_s, pz_r,
    n1_s, n1_r, n2_s, n2_r, n3_s, n3_r, g1_s, g1_r, g2_s, g2_r, g3_s, g3_r, g4_s, g4_r, g5_s,
):
    outer = n_row // inner
    slots, tile = tiles_all.shape[1], tiles_all.shape[2]
    rows_dev, width = cot_ref.shape
    per_dev = rows_dev // tile
    src_tiles = n_col * per_dev
    wide = n_col // near
    col, row = lax.axis_index("col"), lax.axis_index("row")
    out_id, in_id = row // inner, row % inner
    wide_id, near_id = col // near, col % near
    g_rows = width // n_col
    g_piece = g_rows // pieces

    def send(src, dst, s_sem, r_sem, target):
        copy = pltpu.make_async_remote_copy(
            src_ref=src, dst_ref=dst, send_sem=s_sem, recv_sem=r_sem,
            device_id=target, device_id_type=MESH,
        )
        copy.start()

    def sent(ref, s_sem):
        pltpu.make_async_remote_copy(
            src_ref=ref, dst_ref=ref, send_sem=s_sem, recv_sem=s_sem,
            device_id={"col": col}, device_id_type=MESH,
        ).wait_send()

    def landed(ref, r_sem):
        pltpu.make_async_remote_copy(
            src_ref=ref, dst_ref=ref, send_sem=r_sem, recv_sem=r_sem,
            device_id={"col": col}, device_id_type=MESH,
        ).wait_recv()

    def col_at(d):
        return lax.rem(col + d, n_col)

    def row_at(d):
        return lax.rem(row + d, n_row)

    def out_at(d):
        return lax.rem(out_id + d, outer)

    def in_at(d):
        return lax.rem(in_id + d, inner)

    def outer_col(d):
        return lax.rem(wide_id + d, wide) * near + near_id

    def near_col(d):
        return wide_id * near + lax.rem(near_id + d, near)

    def place(j, c):
        return ((c % near) * inner + j) * wide + c // near

    def reducer(r, body):
        if pieces == n_row:
            body()
        else:
            pl.when(r < pieces)(body)

    barrier = pltpu.get_barrier_semaphore()
    each(n_col - 1, lambda d: pl.semaphore_signal(
        barrier, inc=1, device_id={"col": col_at(d + 1)}, device_id_type=MESH))
    each(n_row - 1, lambda d: pl.semaphore_signal(
        barrier, inc=1, device_id={"row": row_at(d + 1)}, device_id_type=MESH))
    index_pairs = ((rows_in, rows_v, rows_ref), (cols_in, cols_v, cols_ref), (count_in, count_v, count_ref))
    fetches = [
        pltpu.make_async_copy(source, target, in_s.at[k])
        for k, (source, target) in enumerate((
            (cot_ref, cot_all.at[out_id]), (feat_in, feat_ref), (tiles_in, tiles_all.at[in_id]),
            (rows_in, rows_v.at[in_id]), (cols_in, cols_v.at[in_id]), (count_in, count_v.at[in_id]),
            (w_in, w_ref),
        ))
    ]
    for fetch in fetches:
        fetch.start()
    own = place(in_id, col)
    fetches[1].wait()
    feat_all[own] = feat_ref[...].astype(BF16)
    fetches[0].wait()
    pl.semaphore_wait(barrier, n_col + n_row - 2)

    def chain(o, step, sems, d):
        send(cot_all.at[o], cot_all.at[o], sems.at[d], cot_r.at[o], {"row": (out_id + step) * inner + in_id})

    if outer > 1:
        pl.when(out_id < outer - 1)(lambda: chain(out_id, 1, up_s, 0))
        pl.when(out_id > 0)(lambda: chain(out_id, -1, down_s, 0))

    def swap(d):
        to = {"row": out_id * inner + in_at(d + 1)}
        send(feat_all.at[own], feat_all.at[own], y_s.at[0, d], feat_r.at[own], to)
        for k, (source, landing, _) in enumerate(index_pairs):
            send(source, landing.at[in_id], y_s.at[k + 1, d], y_r.at[k, in_id], to)
        send(tiles_in, tiles_all.at[in_id], y_s.at[4, d], y_r.at[3, in_id], to)

    each(inner - 1, swap)

    def feat_out(j, e):
        at = place(j, col)
        each(wide - 1, lambda d: send(
            feat_all.at[at], feat_all.at[at], fx_s.at[e, d], feat_r.at[at], {"col": outer_col(d + 1)}))
        each(near - 1, lambda d: send(
            feat_all.at[at], feat_all.at[at], fn_s.at[e, d], feat_r.at[at], {"col": near_col(d + 1)}))

    feat_out(in_id, 0)
    fetches[6].wait()
    weight = w_ref[...]
    w_hi[...] = weight.astype(BF16)
    w_lo[...] = (weight - w_hi[...].astype(F32)).astype(BF16)

    def pass_on(d):
        def from_below():
            o = out_id - d
            landed(cot_all.at[o], cot_r.at[o])
            pl.when(out_id < outer - 1)(lambda: chain(o, 1, up_s, d))

        def from_above():
            o = out_id + d
            landed(cot_all.at[o], cot_r.at[o])
            pl.when(out_id > 0)(lambda: chain(o, -1, down_s, d))

        pl.when(out_id - d >= 0)(from_below)
        pl.when(out_id + d < outer)(from_above)

    def feat_near(j, e):
        def one(d):
            at = place(j, outer_col(d + 1))
            landed(feat_all.at[at], feat_r.at[at])
            each(near - 1, lambda f: send(
                feat_all.at[at], feat_all.at[at], ff_s.at[e, d, f], feat_r.at[at], {"col": near_col(f + 1)}))
        each(wide - 1, one)

    def feat_in_on(e):
        j = in_at(e + 1)
        landed(feat_all.at[place(j, col)], feat_r.at[place(j, col)])
        feat_out(j, e + 1)

    each(inner - 1, feat_in_on)
    if outer > 1:
        pass_on(1)
    feat_near(in_id, 0)

    for fetch in fetches[2:6]:
        fetch.wait()

    def tiles_landed(e):
        j = in_at(e + 1)
        for k, (_, landing, _) in enumerate(index_pairs):
            landed(landing.at[j], y_r.at[k, j])
        landed(tiles_all.at[j], y_r.at[3, j])

    each(inner - 1, tiles_landed)
    moves = [pltpu.make_async_copy(landing, ref, move_s.at[k]) for k, (_, landing, ref) in enumerate(index_pairs)]
    for move in moves:
        move.start()

    def pad_one(t):
        for j in range(inner):
            one = tiles_all[j, t]
            pad[j, t] = one
            pad_t[j, t] = one.T

    each(slots, pad_one)
    for j in range(inner):
        pad[j, slots] = jnp.zeros((tile, tile), BF16)
        pad_t[j, slots] = jnp.zeros((tile, tile), BF16)
    for move in moves:
        move.wait()
    places = [
        [jnp.where(t < count_ref[j, 0, 0], rows_ref[j, 0, 0, t] * src_tiles + cols_ref[j, 0, 0, t], -1)
         for t in range(slots)] for j in range(inner)
    ]

    def lay(o):
        at = o * tile if isinstance(o, int) else pl.multiple_of(o * tile, tile)
        for j in range(inner):
            for k in range(src_tiles):
                index = jnp.int32(slots)
                for t in range(slots):
                    index = jnp.where(places[j][t] == (o * inner + in_id) * src_tiles + k, t, index)
                p = place(j, k)
                a_ref[pl.ds(at, tile), p * tile:(p + 1) * tile] = pad[j, index]
                at_ref[p * tile:(p + 1) * tile, pl.ds(at, tile)] = pad_t[j, index]

    each(outer, lay)
    each(min(outer - 2, 1), lambda d: pass_on(2))
    each(inner - 1, lambda e: feat_near(in_at(e + 1), e + 1))

    def near_landed(j, d):
        def one(e):
            c = lax.rem(wide_id + d, wide) * near + lax.rem(near_id + e + 1, near)
            landed(feat_all.at[place(j, c)], feat_r.at[place(j, c)])
        each(near - 1, one)

    for j in range(inner):
        each(wide, lambda d: near_landed(j, d))

    def project(p, _):
        at = pl.multiple_of(p * rows_dev, rows_dev)
        block = feat_all[p]
        proj[pl.ds(at, rows_dev), :] = (matmul(block, w_hi[...]) + matmul(block, w_lo[...])).astype(BF16)
        feat_t[:, pl.ds(at, rows_dev)] = block.T

    lax.fori_loop(0, inner * n_col, project, None)
    each(outer - 3, lambda d: pass_on(d + 3))

    def forward(d):
        o = out_at(d + 1)
        result = matmul(a_ref[pl.ds(pl.multiple_of(o * tile, tile), tile), :], proj[...])
        if isinstance(d, int) and d == outer - 1:
            part[...] = result
        else:
            part_send[o] = result.astype(BF16)
            send(part_send.at[o], z_in.at[out_id], pz_s.at[d], pz_r.at[out_id], {"row": o * inner + in_id})

    each(outer - 1, forward)
    part[...] = matmul(a_ref[pl.ds(pl.multiple_of(out_id * tile, tile), tile), :], proj[...])

    ax_t[...] = matmul(feat_t[...], at_ref[...]).astype(BF16)
    g_sum[...] = matmul(ax_t[...], cot_all[...].reshape(outer * rows_dev, width))
    g_part[...] = g_sum[...].astype(BF16).reshape(n_col, g_rows, width)

    def g1_out(d):
        c = col_at(d + 1)
        send(g_part.at[c], g1_in.at[col], g1_s.at[d], g1_r.at[col], {"col": c})

    each(n_col - 1, g1_out)

    back[...] = matmul(at_ref[...], cot_all[...].reshape(outer * rows_dev, width)).reshape(back.shape)
    back_send[...] = back[...].astype(BF16)

    def n1_out(d):
        e = lax.rem(near_id + d + 1, near)
        send(back_send.at[e], n1_in.at[near_id], n1_s.at[d], n1_r.at[near_id], {"col": near_col(d + 1)})

    each(near - 1, n1_out)

    def n1_add(d):
        e = lax.rem(near_id + d + 1, near)
        landed(n1_in.at[e], n1_r.at[e])
        back[near_id] += n1_in[e].astype(F32)

    each(near - 1, n1_add)
    n1_sum[...] = back[near_id].astype(BF16)

    def n2_out(d):
        j = in_at(d + 1)
        send(n1_sum.at[j], n2_in.at[in_id], n2_s.at[d], n2_r.at[in_id], {"row": out_id * inner + j})

    each(inner - 1, n2_out)

    gw_part = g_part[col].astype(F32)
    def g1_add(d, total):
        c = col_at(d + 1)
        landed(g1_in.at[c], g1_r.at[c])
        return total + g1_in[c].astype(F32)
    for d in range(n_col - 1):
        gw_part = g1_add(d, gw_part)
    g1_sum[...] = gw_part.astype(BF16).reshape(pieces, g_piece, width)

    def g2_out(d):
        r = row_at(d + 1)
        reducer(r, lambda: send(g1_sum.at[r], g2_in.at[row], g2_s.at[d], g2_r.at[row], {"row": r}))

    each(n_row - 1, g2_out)

    def n2_add(d):
        j = in_at(d + 1)
        landed(n2_in.at[j], n2_r.at[j])
        back[near_id, in_id] += n2_in[j].astype(F32)

    each(inner - 1, n2_add)
    n2_sum[...] = back[near_id, in_id].astype(BF16)

    def n3_out(d):
        w = lax.rem(wide_id + d + 1, wide)
        send(n2_sum.at[w], n3_in.at[wide_id], n3_s.at[d], n3_r.at[wide_id], {"col": outer_col(d + 1)})

    each(wide - 1, n3_out)

    def g2_sum():
        def g2_wait(d):
            r = row_at(d + 1)
            landed(g2_in.at[r], g2_r.at[r])
        each(n_row - 1, g2_wait)
        g2_in[row] = g1_sum[row]
        total = g2_in[0].astype(F32)
        for r in range(1, n_row):
            total = total + g2_in[r].astype(F32)
        gw_all[col, row] = total.astype(BF16)

        def g3_out(d):
            send(gw_all.at[col, row], gw_all.at[col, row], g3_s.at[d], g3_r.at[row], {"row": row_at(d + 1)})
        each(n_row - 1, g3_out)

    reducer(row, g2_sum)

    def to_near(c, r, d):
        def one(e):
            send(gw_all.at[c, r], gw_all.at[c, r], g5_s.at[d, r, e], g4_r.at[c, r], {"col": near_col(e + 1)})
        each(near - 1, one)

    def piece_out(r):
        def one(d):
            send(gw_all.at[col, r], gw_all.at[col, r], g4_s.at[d, r], g4_r.at[col, r], {"col": outer_col(d + 1)})
        each(n_col // near - 1, one)
        to_near(col, r, 0)

    def g3_wait(d):
        r = row_at(d + 1)

        def piece():
            landed(gw_all.at[col, r], g3_r.at[r])
            piece_out(r)
        reducer(r, piece)

    reducer(row, lambda: piece_out(row))
    each(n_row - 1, g3_wait)

    def n3_add(d):
        w = lax.rem(wide_id + d + 1, wide)
        landed(n3_in.at[w], n3_r.at[w])
        back[near_id, in_id, wide_id] += n3_in[w].astype(F32)

    each(wide - 1, n3_add)
    grad_y = back[near_id, in_id, wide_id]
    grad_y = grad_y.astype(BF16)
    gx_ref[...] = matmul(grad_y, w_hi[...], ((1,), (1,))) + matmul(grad_y, w_lo[...], ((1,), (1,)))

    def pass_piece(d):
        c = outer_col(d + 1)

        def one(e):
            r = row_at(e)

            def piece():
                landed(gw_all.at[c, r], g4_r.at[c, r])
                to_near(c, r, d + 1)
            reducer(r, piece)
        each(n_row, one)

    each(n_col // near - 1, pass_piece)

    def z_wait(d):
        o = out_at(d + 1)
        landed(z_in.at[o], pz_r.at[o])
        part[...] += z_in[o].astype(F32)

    each(outer - 1, z_wait)
    agg_ref[...] = part[...].astype(BF16)

    def last_wait(d):
        def one(e):
            c = near_col(e + 1)
            c = lax.rem(c // near + d, n_col // near) * near + c % near
            each(pieces, lambda r: landed(gw_all.at[c, r], g4_r.at[c, r]))
        each(near - 1, one)

    each(n_col // near, last_wait)
    gw_ref[...] = gw_all[...].reshape(width, width)

    def swap_sent(d):
        sent(feat_all.at[0], y_s.at[0, d])
        for k, (source, _, _) in enumerate(index_pairs):
            sent(source, y_s.at[k + 1, d])
        sent(tiles_in, y_s.at[4, d])

    each(inner - 1, swap_sent)
    for j in range(inner):
        each(wide - 1, lambda d: sent(feat_all.at[0], fx_s.at[j, d]))
        each(near - 1, lambda d: sent(feat_all.at[0], fn_s.at[j, d]))
        each(wide - 1, lambda d: each(near - 1, lambda f: sent(feat_all.at[0], ff_s.at[j, d, f])))

    def chain_sent(d):
        def up():
            sent(cot_ref, up_s.at[d])

        def down():
            sent(cot_ref, down_s.at[d])
        pl.when((out_id - d >= 0) & (out_id < outer - 1))(up)
        pl.when((out_id + d < outer) & (out_id > 0))(down)

    if outer > 1:
        each(outer, chain_sent)
    each(outer - 1, lambda d: sent(z_in.at[0], pz_s.at[d]))
    each(near - 1, lambda d: sent(n1_in.at[0], n1_s.at[d]))
    each(inner - 1, lambda d: sent(n2_in.at[0], n2_s.at[d]))
    each(wide - 1, lambda d: sent(n3_in.at[0], n3_s.at[d]))
    each(n_col - 1, lambda d: sent(g1_in.at[0], g1_s.at[d]))
    each(n_row - 1, lambda d: reducer(row_at(d + 1), lambda: sent(g2_in.at[0], g2_s.at[d])))
    reducer(row, lambda: each(n_row - 1, lambda d: sent(g2_in.at[0], g3_s.at[d])))
    each(pieces, lambda r: each(n_col // near - 1, lambda d: sent(g2_in.at[0], g4_s.at[d, r])))
    each(pieces, lambda r: each(n_col // near, lambda d: each(
        near - 1, lambda e: sent(g2_in.at[0], g5_s.at[d, r, e]))))


def write_kernel(agg_ref, gx_ref, gw_ref, agg_out, gx_out, gw_out, agg, gx, narrow, wide, sems):
    loads = [
        pltpu.make_async_copy(source, target, sems.at[k])
        for k, (source, target) in enumerate(((gw_ref, narrow), (agg_ref, agg), (gx_ref, gx)))
    ]
    stores = [
        pltpu.make_async_copy(source, target, sems.at[3 + k])
        for k, (source, target) in enumerate(((wide, gw_out), (agg, agg_out), (gx, gx_out)))
    ]
    for load in loads:
        load.start()
    for k in (1, 2):
        loads[k].wait()
        stores[k].start()
    loads[0].wait()
    wide[...] = narrow[...].astype(F32)
    for k in (0, 1, 2):
        if k == 0:
            stores[k].start()
        stores[k].wait()


def shards(n_col, n_row, features, weight, tiles, tile_rows, tile_cols, tile_count, cotangent):
    slots, tile = tiles.shape[2], tiles.shape[-1]
    rows_dev, width = features.shape
    inner = 2 if n_row % 2 == 0 else 1
    near = 2 if n_col % 2 == 0 else 1
    outer = n_row // inner
    g_rows = width // n_col
    pieces = min(n_row, g_rows // 16)
    g_piece = g_rows // pieces
    pair, half, wide = inner * n_col * rows_dev, outer * rows_dev, n_col // near
    dma = pltpu.SemaphoreType.DMA
    vmem = pl.BlockSpec(memory_space=pltpu.VMEM)
    hbm = pl.BlockSpec(memory_space=pltpu.HBM)
    anywhere = pl.BlockSpec(memory_space=pl.ANY)
    buffers = [
        (features.shape, F32),
        (weight.shape, F32),
        ((inner, *tiles.shape[2:]), BF16),
        ((inner * n_col, rows_dev, width), BF16),
        ((width, pair), BF16),
        ((width, half), BF16),
        ((outer, rows_dev, width), BF16),
        ((inner, slots + 1, tile, tile), BF16),
        ((inner, slots + 1, tile, tile), BF16),
        ((half, pair), BF16),
        ((pair, half), BF16),
        ((width, width), BF16),
        ((width, width), BF16),
        ((pair, width), BF16),
        ((rows_dev, width), F32),
        ((outer, rows_dev, width), BF16),
        ((outer, rows_dev, width), BF16),
        ((near, inner, wide, rows_dev, width), F32),
        ((near, inner, wide, rows_dev, width), BF16),
        ((near, inner, wide, rows_dev, width), BF16),
        ((inner, wide, rows_dev, width), BF16),
        ((inner, wide, rows_dev, width), BF16),
        ((wide, rows_dev, width), BF16),
        ((wide, rows_dev, width), BF16),
        ((width, width), F32),
        ((n_col, g_rows, width), BF16),
        ((n_col, g_rows, width), BF16),
        ((pieces, g_piece, width), BF16),
        ((n_row, g_piece, width), BF16),
        ((n_col, pieces, g_piece, width), BF16),
    ]
    held = sum(math.prod(shape) * jnp.dtype(kind).itemsize for shape, kind in buffers)
    limit = max(56 * 2**20, min(held + 12 * 2**20, 63 * 2**20))
    sems = [
        (7,), (3,), (5, inner), (4, inner), (inner, wide), (inner, near), (inner, wide, near),
        (inner * n_col,), (outer,), (outer,), (outer,), (outer,), (outer,),
        (near,), (near,), (inner,), (inner,), (wide,), (wide,), (n_col,), (n_col,), (n_row,), (n_row,),
        (n_row,), (n_row,), (n_col, pieces), (n_col, pieces), (n_col, pieces, near),
    ]
    aggregated, grad_x, grad_w = pl.pallas_call(
        functools.partial(layer_kernel, n_col, n_row, inner, near, pieces),
        out_shape=(
            jax.ShapeDtypeStruct((rows_dev, width), BF16),
            jax.ShapeDtypeStruct((rows_dev, width), F32),
            jax.ShapeDtypeStruct((width, width), BF16),
        ),
        in_specs=[hbm] * 7,
        out_specs=(vmem, vmem, vmem),
        scratch_shapes=[
            kind((inner, *one.shape), jnp.int32)
            for kind in (pltpu.SMEM, pltpu.VMEM) for one in (tile_rows, tile_cols, tile_count)
        ]
        + [pltpu.VMEM(shape, kind) for shape, kind in buffers] + [dma(s) for s in sems],
        compiler_params=pltpu.CompilerParams(
            collective_id=0, has_side_effects=True, vmem_limit_bytes=limit
        ),
        name="layer",
    )(
        tile_rows, tile_cols, tile_count,
        features, weight, tiles[0, 0], cotangent,
    )
    return pl.pallas_call(
        write_kernel,
        out_shape=(
            jax.ShapeDtypeStruct((rows_dev, width), BF16),
            jax.ShapeDtypeStruct((rows_dev, width), F32),
            jax.ShapeDtypeStruct((width, width), F32),
        ),
        in_specs=[anywhere] * 3,
        out_specs=(hbm,) * 3,
        scratch_shapes=[
            pltpu.VMEM((rows_dev, width), BF16), pltpu.VMEM((rows_dev, width), F32),
            pltpu.VMEM((width, width), BF16), pltpu.VMEM((width, width), F32), dma((6,)),
        ],
        compiler_params=pltpu.CompilerParams(vmem_limit_bytes=limit),
        name="write",
    )(aggregated, grad_x, grad_w)


def solution(mesh):
    placed = (
        P(("row", "col"), None),
        P(),
        P("col", "row", None, None, None),
        P("col", "row", None),
        P("col", "row", None),
        P("col", "row"),
        P(("col", "row"), None),
    )
    return jax.shard_map(
        functools.partial(shards, mesh.shape["col"], mesh.shape["row"]),
        mesh=mesh,
        in_specs=placed,
        out_specs=(P(("col", "row"), None), P(("row", "col"), None), P()),
        check_vma=False,
    )
```

time: 54.6 us -> 50.1 us (0.918)
  Pallas kernels: 53.1 us -> 48.7 us
    pallas_call x1, Pallas kernels: 50.9 us -> 46.4 us  [shards(): pl.pallas_call(functools.partial(layer_kernel, n_col, n_row, inner, near,...]
where the time goes in v6:
time: 50.1 us; the launch traced here: 49.9 us
  Pallas kernels  48.7 us (97%)
  between operations  1.29 us (3%)
    pallas_call x1, Pallas kernels, shards(): pl.pallas_call(functools.partial(layer_kernel, n_col, n_row, inner, near,...  46.4 us
    pallas_call x1, Pallas kernels, shards(): pl.pallas_call(write_kernel, out_shape=(jax.ShapeDtypeStruct((rows_dev, w...  2.26 us

profile of v6, /device:TPU:1, one launch (start us, length us, event | category | flops | bytes accessed | tf_op | source)
XLA Modules:
  0.0 49.9 jit_solution(840581376262542912)
XLA Ops:
  1.3 46.4 %layer.1 = (bf16[128,512]{1,0:T(8,128)(2,1)}, f32[128,512]{1,0:T(8,128)}, bf16[512,512]{1,0:T(8,128)(2,1)}) custom-call(s32[1,1,6]{2,1,0:T(1,128)} %rows_in.1, s32[1,1,6]{2,1,0:T(1,128)} %cols_in.1, s32[1,1]{1,0:T(1,128)S(6)} %copy.10.count_in, f32[128,512]{1,0:T(8,128)} %feat_in.1, f32[512,512]{1,0:T(8,128)} %w_in.1, bf16[6,128,128]{2,1,0:T(8,128)(2,1)} %bitcast.1, ...), custom_call_target="tpu_custom_call" | custom-call | tf_op jit(solution)/shard_map/layer/pallas_call | solution.py:509
  47.7 2.3 %write.1 = (bf16[128,512]{1,0:T(8,128)(2,1)}, f32[128,512]{1,0:T(8,128)}, f32[512,512]{1,0:T(8,128)}) custom-call(bf16[128,512]{1,0:T(8,128)(2,1)} %get-tuple-element.6.agg_ref, f32[128,512]{1,0:T(8,128)} %get-tuple-element.7.gx_ref, bf16[512,512]{1,0:T(8,128)(2,1)} %get-tuple-element.8.gw_ref), custom_call_target="tpu_custom_call" | custom-call | tf_op jit(solution)/shard_map/write/pallas_call | solution.py:531

commit v7 on v6

--- a/solution.py
+++ b/solution.py
@@ -31,7 +31,7 @@
     agg_ref, gx_ref, gw_ref,
     rows_ref, cols_ref, count_ref, rows_v, cols_v, count_v, feat_ref, w_ref, tiles_all,
     feat_all, feat_t, ax_t, cot_all, pad, pad_t, a_ref, at_ref, w_hi, w_lo, proj, part, part_send, z_in,
-    back, back_send, n1_in, n1_sum, n2_in, n2_sum, n3_in, g_sum, g_part, g1_in, g1_sum, g2_in, gw_all,
+    back, back_send, n1_in, n1_sum, n2_in, n2_sum, n3_in, g_part, g1_in, g1_sum, g2_in, gw_all,
     in_s, move_s, y_s, y_r, fx_s, fn_s, ff_s, feat_r, up_s, down_s, cot_r, pz_s, pz_r,
     n1_s, n1_r, n2_s, n2_r, n3_s, n3_r, g1_s, g1_r, g2_s, g2_r, g3_s, g3_r, g4_s, g4_r, g5_s,
 ):
@@ -220,7 +220,6 @@
 
     each(outer, lay)
     each(min(outer - 2, 1), lambda d: pass_on(2))
-    each(inner - 1, lambda e: feat_near(in_at(e + 1), e + 1))
 
     def near_landed(j, d):
         def one(e):
@@ -228,39 +227,53 @@
             landed(feat_all.at[place(j, c)], feat_r.at[place(j, c)])
         each(near - 1, one)
 
-    for j in range(inner):
-        each(wide, lambda d: near_landed(j, d))
-
-    def project(p, _):
-        at = pl.multiple_of(p * rows_dev, rows_dev)
-        block = feat_all[p]
-        proj[pl.ds(at, rows_dev), :] = (matmul(block, w_hi[...]) + matmul(block, w_lo[...])).astype(BF16)
-        feat_t[:, pl.ds(at, rows_dev)] = block.T
-
-    lax.fori_loop(0, inner * n_col, project, None)
+    def project(j):
+        def one(c, _):
+            p = place(j, c)
+            block = feat_all[p]
+            proj[pl.ds(pl.multiple_of(p * rows_dev, rows_dev), rows_dev), :] = (
+                matmul(block, w_hi[...]) + matmul(block, w_lo[...])
+            ).astype(BF16)
+        lax.fori_loop(0, n_col, one, None)
+
+    def turn(j):
+        def one(c, _):
+            p = place(j, c)
+            feat_t[:, pl.ds(pl.multiple_of(p * rows_dev, rows_dev), rows_dev)] = feat_all[p].T
+        lax.fori_loop(0, n_col, one, None)
+
+    each(wide, lambda d: near_landed(in_id, d))
+    turn(in_id)
+    project(in_id)
+    each(inner - 1, lambda e: feat_near(in_at(e + 1), e + 1))
+    for e in range(1, inner):
+        each(wide, lambda d: near_landed(in_at(e), d))
+        turn(in_at(e))
+
+    ax_t[...] = matmul(feat_t[...], at_ref[...]).astype(BF16)
     each(outer - 3, lambda d: pass_on(d + 3))
-
-    def forward(d):
-        o = out_at(d + 1)
-        result = matmul(a_ref[pl.ds(pl.multiple_of(o * tile, tile), tile), :], proj[...])
-        if isinstance(d, int) and d == outer - 1:
-            part[...] = result
-        else:
-            part_send[o] = result.astype(BF16)
-            send(part_send.at[o], z_in.at[out_id], pz_s.at[d], pz_r.at[out_id], {"row": o * inner + in_id})
-
-    each(outer - 1, forward)
-    part[...] = matmul(a_ref[pl.ds(pl.multiple_of(out_id * tile, tile), tile), :], proj[...])
-
-    ax_t[...] = matmul(feat_t[...], at_ref[...]).astype(BF16)
-    g_sum[...] = matmul(ax_t[...], cot_all[...].reshape(outer * rows_dev, width))
-    g_part[...] = g_sum[...].astype(BF16).reshape(n_col, g_rows, width)
+    g_part[...] = matmul(
+        ax_t[...], cot_all[...].reshape(outer * rows_dev, width)
+    ).astype(BF16).reshape(n_col, g_rows, width)
 
     def g1_out(d):
         c = col_at(d + 1)
         send(g_part.at[c], g1_in.at[col], g1_s.at[d], g1_r.at[col], {"col": c})
 
     each(n_col - 1, g1_out)
+
+    for e in range(1, inner):
+        project(in_at(e))
+
+    def forward(d):
+        o = out_at(d + 1)
+        part_send[o] = matmul(
+            a_ref[pl.ds(pl.multiple_of(o * tile, tile), tile), :], proj[...]
+        ).astype(BF16)
+        send(part_send.at[o], z_in.at[out_id], pz_s.at[d], pz_r.at[out_id], {"row": o * inner + in_id})
+
+    each(outer - 1, forward)
+    part[...] = matmul(a_ref[pl.ds(pl.multiple_of(out_id * tile, tile), tile), :], proj[...])
 
     back[...] = matmul(at_ref[...], cot_all[...].reshape(outer * rows_dev, width)).reshape(back.shape)
     back_send[...] = back[...].astype(BF16)
@@ -491,7 +504,6 @@
         ((inner, wide, rows_dev, width), BF16),
         ((wide, rows_dev, width), BF16),
         ((wide, rows_dev, width), BF16),
-        ((width, width), F32),
         ((n_col, g_rows, width), BF16),
         ((n_col, g_rows, width), BF16),
         ((pieces, g_piece, width), BF16),

time: 50.1 us -> 52 us (1.038)
  Pallas kernels: 48.7 us -> 50.6 us
    pallas_call x1, Pallas kernels: 46.4 us -> 48.3 us  [shards(): pl.pallas_call(functools.partial(layer_kernel, n_col, n_row, inner, near,...]
where the time goes in v7:
time: 52 us; the launch traced here: 51.9 us
  Pallas kernels  50.6 us (97%)
  between operations  1.29 us (2%)
    pallas_call x1, Pallas kernels, shards(): pl.pallas_call(functools.partial(layer_kernel, n_col, n_row, inner, near,...  48.3 us
    pallas_call x1, Pallas kernels, shards(): pl.pallas_call(write_kernel, out_shape=(jax.ShapeDtypeStruct((rows_dev, w...  2.26 us

profile of v7, /device:TPU:1, one launch (start us, length us, event | category | flops | bytes accessed | tf_op | source)
XLA Modules:
  0.0 51.9 jit_solution(13758718224607934437)
XLA Ops:
  1.3 48.3 %layer.1 = (bf16[128,512]{1,0:T(8,128)(2,1)}, f32[128,512]{1,0:T(8,128)}, bf16[512,512]{1,0:T(8,128)(2,1)}) custom-call(s32[1,1,6]{2,1,0:T(1,128)} %rows_in.1, s32[1,1,6]{2,1,0:T(1,128)} %cols_in.1, s32[1,1]{1,0:T(1,128)S(6)} %copy.10.count_in, f32[128,512]{1,0:T(8,128)} %feat_in.1, f32[512,512]{1,0:T(8,128)} %w_in.1, bf16[6,128,128]{2,1,0:T(8,128)(2,1)} %bitcast.1, ...), custom_call_target="tpu_custom_call" | custom-call | tf_op jit(solution)/shard_map/layer/pallas_call | solution.py:521
  49.6 2.3 %write.1 = (bf16[128,512]{1,0:T(8,128)(2,1)}, f32[128,512]{1,0:T(8,128)}, f32[512,512]{1,0:T(8,128)}) custom-call(bf16[128,512]{1,0:T(8,128)(2,1)} %get-tuple-element.6.agg_ref, f32[128,512]{1,0:T(8,128)} %get-tuple-element.7.gx_ref, bf16[512,512]{1,0:T(8,128)(2,1)} %get-tuple-element.8.gw_ref), custom_call_target="tpu_custom_call" | custom-call | tf_op jit(solution)/shard_map/write/pallas_call | solution.py:543

commit v8 on v7

--- a/solution.py
+++ b/solution.py
@@ -250,20 +250,10 @@
         each(wide, lambda d: near_landed(in_at(e), d))
         turn(in_at(e))
 
-    ax_t[...] = matmul(feat_t[...], at_ref[...]).astype(BF16)
-    each(outer - 3, lambda d: pass_on(d + 3))
-    g_part[...] = matmul(
-        ax_t[...], cot_all[...].reshape(outer * rows_dev, width)
-    ).astype(BF16).reshape(n_col, g_rows, width)
-
-    def g1_out(d):
-        c = col_at(d + 1)
-        send(g_part.at[c], g1_in.at[col], g1_s.at[d], g1_r.at[col], {"col": c})
-
-    each(n_col - 1, g1_out)
-
     for e in range(1, inner):
         project(in_at(e))
+
+    each(outer - 3, lambda d: pass_on(d + 3))
 
     def forward(d):
         o = out_at(d + 1)
@@ -274,6 +264,17 @@
 
     each(outer - 1, forward)
     part[...] = matmul(a_ref[pl.ds(pl.multiple_of(out_id * tile, tile), tile), :], proj[...])
+
+    ax_t[...] = matmul(feat_t[...], at_ref[...]).astype(BF16)
+    g_part[...] = matmul(
+        ax_t[...], cot_all[...].reshape(outer * rows_dev, width)
+    ).astype(BF16).reshape(n_col, g_rows, width)
+
+    def g1_out(d):
+        c = col_at(d + 1)
+        send(g_part.at[c], g1_in.at[col], g1_s.at[d], g1_r.at[col], {"col": c})
+
+    each(n_col - 1, g1_out)
 
     back[...] = matmul(at_ref[...], cot_all[...].reshape(outer * rows_dev, width)).reshape(back.shape)
     back_send[...] = back[...].astype(BF16)

time: 52 us -> 50.8 us (0.977)
  Pallas kernels: 50.6 us -> 49.4 us
    pallas_call x1, Pallas kernels: 48.3 us -> 47.1 us  [shards(): pl.pallas_call(functools.partial(layer_kernel, n_col, n_row, inner, near,...]
where the time goes in v8:
time: 50.8 us; the launch traced here: 50.7 us
  Pallas kernels  49.4 us (97%)
  between operations  1.29 us (3%)
    pallas_call x1, Pallas kernels, shards(): pl.pallas_call(functools.partial(layer_kernel, n_col, n_row, inner, near,...  47.1 us
    pallas_call x1, Pallas kernels, shards(): pl.pallas_call(write_kernel, out_shape=(jax.ShapeDtypeStruct((rows_dev, w...  2.26 us

profile of v8, /device:TPU:1, one launch (start us, length us, event | category | flops | bytes accessed | tf_op | source)
XLA Modules:
  0.0 50.7 jit_solution(15410677969041095507)
XLA Ops:
  1.3 47.1 %layer.1 = (bf16[128,512]{1,0:T(8,128)(2,1)}, f32[128,512]{1,0:T(8,128)}, bf16[512,512]{1,0:T(8,128)(2,1)}) custom-call(s32[1,1,6]{2,1,0:T(1,128)} %rows_in.1, s32[1,1,6]{2,1,0:T(1,128)} %cols_in.1, s32[1,1]{1,0:T(1,128)S(6)} %copy.10.count_in, f32[128,512]{1,0:T(8,128)} %feat_in.1, f32[512,512]{1,0:T(8,128)} %w_in.1, bf16[6,128,128]{2,1,0:T(8,128)(2,1)} %bitcast.1, ...), custom_call_target="tpu_custom_call" | custom-call | tf_op jit(solution)/shard_map/layer/pallas_call | solution.py:522
  48.4 2.3 %write.1 = (bf16[128,512]{1,0:T(8,128)(2,1)}, f32[128,512]{1,0:T(8,128)}, f32[512,512]{1,0:T(8,128)}) custom-call(bf16[128,512]{1,0:T(8,128)(2,1)} %get-tuple-element.6.agg_ref, f32[128,512]{1,0:T(8,128)} %get-tuple-element.7.gx_ref, bf16[512,512]{1,0:T(8,128)(2,1)} %get-tuple-element.8.gw_ref), custom_call_target="tpu_custom_call" | custom-call | tf_op jit(solution)/shard_map/write/pallas_call | solution.py:544
